TPU v7x, 256 devices: a whole 4x4x8 slice. The times are simulated.
256 devices in a mesh: seg: 64 (over y, z, core), head: 4 (over x).
Axes of the slice: x: 4, y: 4, z: 8, core: 2. Of those that a mesh axis runs over, the one named last changes fastest.
Arguments:
- queries: bfloat16 [16384, 2048], P('seg', 'head'), may hold values from -20 to 20
- keys: bfloat16 [16384, 2048], P('seg', 'head'), may hold values from -12 to 12
- values: bfloat16 [16384, 2048], P('seg', 'head'), may hold values from -6 to 6
- out_grad: bfloat16 [16384, 2048], P('seg', 'head'), may hold values from -5 to 5
- out_weight: bfloat16 [2048, 2048], P('head'), may hold values from -1 to 1
- retr_owner: int32 [64, 32], replicated, may hold values from 0 to 63, as said below
- retr_block: int32 [64, 32], replicated, may hold values from -1 to 1, as said below
Outputs:
- layer_out: bfloat16 [16384, 2048], P('seg', 'head')
- query_grad: bfloat16 [16384, 2048], P('seg', 'head')
- key_grad: bfloat16 [16384, 2048], P('seg', 'head')
- value_grad: bfloat16 [16384, 2048], P('seg', 'head')
- proj_grad_t: float32 [2048, 2048], P('seg', 'head')
Inputs may be any that keep to these rules, and one draw needn't show every extreme that they name: `retr_owner`: row s lists 32 owners, all different from one another and from s. `retr_block`: padding (-1) comes after the live entries of a row; every row has at least 24 live entries.
All inputs are finite; a program needn't handle non-finite values.
Results may differ from a plain program's by a relative error of at most 0.012.
Values may be sent and summed in bfloat16 or wider, within the bound.
A program may use at most 128 MiB of HBM per device.

v0:
```python
import math

import jax
import jax.numpy as jnp
from jax import lax
from jax.sharding import PartitionSpec as P

DH = 128
BLOCK = 128


def shifted(block, axis, distance):
    devices = range(lax.axis_size(axis))
    route = [(i - distance, i) for i in devices if i - distance in devices]
    return lax.ppermute(block, axis, route)


def split_heads(tok_rows, count):
    return tok_rows.reshape(tok_rows.shape[0], count, -1).transpose(1, 0, 2)


def join_heads(stacked):
    return stacked.transpose(1, 0, 2).reshape(stacked.shape[1], -1)


def product(form, left_side, right_side):
    return jnp.einsum(form, left_side, right_side, preferred_element_type=jnp.float32)


def attend(packed, mem_live, has_cache, score_scale):
    queries, keys, values, cache_k, cache_v, mem_k, mem_v, d_attn = packed
    length = queries.shape[1]
    causal = jnp.arange(length)[:, None] >= jnp.arange(length)[None, :]
    own = jnp.where(causal[None], product("hqd,hkd->hqk", queries, keys) * score_scale, -jnp.inf)
    cached = jnp.where(has_cache, product("hqd,hkd->hqk", queries, cache_k) * score_scale, -jnp.inf)
    stored = jnp.where(
        mem_live[None, None, :], product("hqd,hkd->hqk", queries, mem_k) * score_scale, -jnp.inf
    )
    row_top = jnp.maximum(jnp.maximum(jnp.max(own, -1), jnp.max(cached, -1)), jnp.max(stored, -1))[
        ..., None
    ]
    row_total = (
        jnp.sum(jnp.exp(own - row_top), -1)
        + jnp.sum(jnp.exp(cached - row_top), -1)
        + jnp.sum(jnp.exp(stored - row_top), -1)
    )
    log_total = row_top + jnp.log(row_total)[..., None]
    weights = [jnp.exp(group_scores - log_total) for group_scores in (own, cached, stored)]
    rounded = [entry.astype(jnp.bfloat16) for entry in weights]
    sources = (values, cache_v, mem_v)
    mixed_sum = (
        product("hqk,hkd->hqd", rounded[0], sources[0])
        + product("hqk,hkd->hqd", rounded[1], sources[1])
        + product("hqk,hkd->hqd", rounded[2], sources[2])
    )
    attn = mixed_sum.astype(jnp.bfloat16)
    row_delta = jnp.sum(d_attn.astype(jnp.float32) * attn.astype(jnp.float32), -1)[..., None]
    slopes = [
        (entry * (product("hqd,hkd->hqk", d_attn, source) - row_delta)).astype(jnp.bfloat16)
        for entry, source in zip(weights, sources)
    ]
    grad_q = score_scale * (
        product("hqk,hkd->hqd", slopes[0], keys)
        + product("hqk,hkd->hqd", slopes[1], cache_k)
        + product("hqk,hkd->hqd", slopes[2], mem_k)
    )
    grad_k = score_scale * product("hqk,hqd->hkd", slopes[0], queries)
    grad_v = product("hqk,hqd->hkd", rounded[0], d_attn)
    grad_k_cache = score_scale * product("hqk,hqd->hkd", slopes[1], queries)
    grad_v_cache = product("hqk,hqd->hkd", rounded[1], d_attn)
    return (
        attn,
        grad_q,
        grad_k,
        grad_v,
        grad_k_cache,
        grad_v_cache,
        log_total[..., 0],
        row_delta[..., 0],
    )


def per_device(queries, keys, values, out_grad, out_weight, retr_owner, retr_block):
    my_index = lax.axis_index("seg")
    tok_count = queries.shape[0]
    full_width = queries.shape[1]
    head_dev = full_width // DH
    per_group = 2
    group_count = head_dev // per_group
    score_scale = 1.0 / math.sqrt(DH)
    cache_k, cache_v = shifted((keys, values), "seg", 1)
    matches = (retr_owner == my_index) & (retr_block >= 0)
    wanted = jnp.sum(jnp.where(matches, retr_block, 0), axis=1)
    served = jnp.any(matches, axis=1)[:, None, None]
    key_blocks = keys.reshape(tok_count // BLOCK, BLOCK, full_width)
    value_blocks = values.reshape(tok_count // BLOCK, BLOCK, full_width)
    zero_fill = jnp.zeros((), keys.dtype)
    send_k = jnp.where(served, key_blocks[wanted], zero_fill)
    send_v = jnp.where(served, value_blocks[wanted], zero_fill)
    recv_k, recv_v = (
        lax.all_to_all(send_k, "seg", split_axis=0, concat_axis=0, tiled=True),
        lax.all_to_all(send_v, "seg", split_axis=0, concat_axis=0, tiled=True),
    )
    my_owner = lax.dynamic_index_in_dim(retr_owner, my_index, 0, False)
    my_block = lax.dynamic_index_in_dim(retr_block, my_index, 0, False)
    mem_k = recv_k[my_owner].reshape(-1, full_width)
    mem_v = recv_v[my_owner].reshape(-1, full_width)
    mem_live = jnp.repeat(my_block >= 0, BLOCK)
    full_grad = lax.all_gather(out_grad, "head", axis=1, tiled=True)
    d_attn = lax.dot_general(
        full_grad, out_weight, (((1,), (1,)), ((), ())), preferred_element_type=jnp.float32
    ).astype(jnp.bfloat16)

    def grouped(tok_rows):
        stacked = split_heads(tok_rows, head_dev)
        return stacked.reshape(group_count, per_group, stacked.shape[1], stacked.shape[2])

    packed = tuple(
        (
            grouped(entry)
            for entry in (queries, keys, values, cache_k, cache_v, mem_k, mem_v, d_attn)
        )
    )
    results = lax.map(
        lambda group_args: attend(group_args, mem_live, my_index > 0, score_scale), packed
    )

    def ungrouped(stacked):
        return join_heads(stacked.reshape(head_dev, stacked.shape[2], stacked.shape[3]))

    attn_rows = ungrouped(results[0])
    grad_q = ungrouped(results[1])
    grad_k = ungrouped(results[2])
    grad_v = ungrouped(results[3])
    partial_out = jnp.dot(attn_rows, out_weight, preferred_element_type=jnp.float32)
    layer_out = lax.psum_scatter(
        partial_out.astype(jnp.bfloat16), "head", scatter_dimension=1, tiled=True
    )
    proj_grad_t = lax.psum_scatter(
        lax.dot_general(
            full_grad, attn_rows, (((0,), (0,)), ((), ())), preferred_element_type=jnp.float32
        ),
        "seg",
        scatter_dimension=0,
        tiled=True,
    )
    carried_k, carried_v = (
        shifted(ungrouped(results[4]).astype(jnp.bfloat16), "seg", -1).astype(jnp.float32),
        shifted(ungrouped(results[5]).astype(jnp.bfloat16), "seg", -1).astype(jnp.float32),
    )
    query_grad = grad_q.astype(jnp.bfloat16)
    key_grad = (grad_k + carried_k).astype(jnp.bfloat16)
    value_grad = (grad_v + carried_v).astype(jnp.bfloat16)
    return (layer_out, query_grad, key_grad, value_grad, proj_grad_t)


def solution(mesh):
    in_specs = (
        P("seg", "head"),
        P("seg", "head"),
        P("seg", "head"),
        P("seg", "head"),
        P("head", None),
        P(),
        P(),
    )
    out_specs = (
        P("seg", "head"),
        P("seg", "head"),
        P("seg", "head"),
        P("seg", "head"),
        P("seg", "head"),
    )
    return jax.shard_map(
        per_device, mesh=mesh, in_specs=in_specs, out_specs=out_specs, check_vma=False
    )
```

profile of v0, /device:TPU:1, one launch (start us, length us, event | category | flops | bytes accessed | tf_op | source)
XLA Modules:
  0.0 716.5 jit_solution(5851117078718787191)
XLA Ops:
  7.2 0.9 fusion.102
  8.9 6.3 gather_fusion
  15.2 5.3 gather_fusion.2
  20.5 9.2 %broadcast_select_fusion = (bf16[64,128,512]{2,1,0:T(8,128)(2,1)}, bf16[64,128,512]{2,1,0:T(8,128)(2,1)S(1)}) fusion(bf16[64,128,512]{2,1,0:T(8,128)(2,1)} %gather_fusion.2, pred[64]{0:T(512)(128)(4,1)S(1)} %get-tuple-element.353, bf16[64,128,512]{2,1,0:T(8,128)(2,1)} %gather_fusion), kind=kLoop, calls=%fused_computation.114 | loop fusion | flops 8388608 | bytes 33554496 | tf_op jit(solution)/shard_map/jit(_where)/select_n | solution.py:99
  29.7 199.1 %all_to_all.10 = bf16[64,128,512]{2,1,0:T(8,128)(2,1)} all-to-all(bf16[64,128,512]{2,1,0:T(8,128)(2,1)S(1)} %get-tuple-element.364), channel_id=1, replica_groups=mesh['seg'=64,'head'=4] {'seg'}, dimensions={0} | all-to-all | bytes 16777216 | tf_op jit(solution)/shard_map/all_to_all | solution.py:101
  228.8 6.1 all-to-all-start.1
  235.7 3.5 collective-permute-start.1
  239.3 2.1 collective-permute-start
  244.1 174.0 %collective-permute-done.1 = bf16[256,512]{1,0:T(8,128)(2,1)S(1)} collective-permute-done((bf16[256,512]{1,0:T(8,128)(2,1)S(1)}, bf16[256,512]{1,0:T(8,128)(2,1)S(1)}, u32[]{:S(2)}, u32[]{:S(2)}) %collective-permute-start.1) | collective-permute-done | bytes 262176 | tf_op jit(solution)/shard_map/ppermute | solution.py:15
  419.0 1.9 collective-permute-done
  421.7 2.0 convolution_convert_fusion.1
  423.7 0.9 copy.113
  424.6 6.2 gather_fusion.1
  430.8 6.9 reshape.234
  437.7 4.7 copy.136
  442.4 6.2 gather_fusion.3
  448.5 6.9 reshape_reshape.7
  455.5 7.5 %copy.112 = bf16[4,4096,128]{1,2,0:T(8,128)(2,1)} copy(bf16[4,4096,128]{2,0,1:T(4,128)(2,1)} %bitcast.267) | data formatting | bytes 8388608 | tf_op jit(solution)/shard_map/transpose | solution.py:19
  463.0 72.7 %while.23 = (s32[]{:T(128)}, bf16[2,2,256,128]{2,3,1,0:T(8,128)(2,1)}, bf16[2,2,256,128]{3,2,1,0:T(8,128)(2,1)}, f32[2,2,256,128]{3,2,1,0:T(8,128)}, f32[2,2,256...) while((s32[]{:T(128)}, ...), condition=%wide.region_10.11_spmd.clone, body=%wide.region_2.10_spmd.clone.sunk | while | flops 2577464320 | bytes 106643744 | solution.py:124
  463.1 3.0 fusion.179
  466.1 1.5 fusion.181
  467.6 1.5 fusion.180
  469.4 1.3 exponential_reduce_fusion.5
  470.7 1.1 fusion.183
  471.8 1.9 fusion.182
  473.7 1.8 bitcast_dynamic-update-slice_fusion.2
  475.5 1.0 multiply_reduce_fusion.2
  476.5 1.2 fusion.187
  478.4 1.8 fusion.191
  480.2 1.2 fusion.185
  481.5 1.9 fusion.186
  483.4 8.4 %fusion.184 = f32[2,256,128]{2,1,0:T(8,128)} fusion(bf16[2,2,4096,128]{3,2,1,0:T(8,128)(2,1)} %get-tuple-element.535, s32[]{:T(128)} %get-tuple-element.506, f32[2,256,4096]{2,1,0:T(8,128)} %copy-done.1, f32[2,256]{1,0:T(2,128)S(1)} %multiply_reduce_fusion.2, f32[2,256]{1,0:T(2,128)S(1)} %log_add_fusion.2, ...), kind=kOutput, calls=%fused_computation.14.clone.1 | convolution fusion | flops 1082130432 | bytes 12981760 | tf_op jit(solution)/shard_map/while/body/eval_jaxpr/hqk,hkd->hqd/dot_general | solution.py:27
  491.8 2.1 fusion.188
  493.9 1.8 fusion.189
  495.7 1.8 fusion.190
  497.5 1.8 fusion.192
  499.4 3.0 fusion.179
  502.4 1.5 fusion.181
  504.0 1.5 fusion.180
  505.7 1.3 exponential_reduce_fusion.5
  507.0 1.1 fusion.183
  508.2 1.9 fusion.182
  510.1 1.8 bitcast_dynamic-update-slice_fusion.2
  511.9 1.0 multiply_reduce_fusion.2
  512.8 1.2 fusion.187
  514.8 1.8 fusion.191
  516.6 1.2 fusion.185
  517.8 1.9 fusion.186
  519.7 8.4 %fusion.184 = f32[2,256,128]{2,1,0:T(8,128)} fusion(bf16[2,2,4096,128]{3,2,1,0:T(8,128)(2,1)} %get-tuple-element.535, s32[]{:T(128)} %get-tuple-element.506, f32[2,256,4096]{2,1,0:T(8,128)} %copy-done.1, f32[2,256]{1,0:T(2,128)S(1)} %multiply_reduce_fusion.2, f32[2,256]{1,0:T(2,128)S(1)} %log_add_fusion.2, ...), kind=kOutput, calls=%fused_computation.14.clone.1 | convolution fusion | flops 1082130432 | bytes 12981760 | tf_op jit(solution)/shard_map/while/body/eval_jaxpr/hqk,hkd->hqd/dot_general | solution.py:27
  528.1 2.1 fusion.188
  530.2 1.8 fusion.189
  532.0 1.9 fusion.190
  533.9 1.8 fusion.192
  535.7 2.8 convolution_convert_fusion
  538.6 3.6 convolution_bitcast_fusion.2
  542.2 5.3 copy.139
  547.6 0.9 copy-done.10
  548.8 1.9 collective-permute-start.3
  550.7 1.2 copy.117
  551.9 1.9 collective-permute-start.2
  555.5 2.1 collective-permute-done.3
  558.4 2.4 collective-permute-done.2
  561.6 3.4 reduce-scatter.5.cloned.1.call-done
  565.0 145.0 %reduce-scatter.7.cloned.1.call-done = f32[32,512]{1,0:T(8,128)} async-done(((f32[2048,512]{1,0:T(8,128)}), f32[32,512]{1,0:T(8,128)}) %reduce-scatter.7.cloned.1.call-update) | async-done | bytes 65552
  (79 shorter events, 11.5 us)
Async XLA Ops:
  7.2 414.5 %copy-start = (bf16[512,2048]{1,0:T(8,128)(2,1)S(1)}, bf16[512,2048]{1,0:T(8,128)(2,1)}, u32[]{:S(2)}) copy-start(bf16[512,2048]{1,0:T(8,128)(2,1)} %param.13) | copy-start | bytes 6291460
  8.8 6.3 copy-start.2
  228.8 10.5 %copy-start.3 = (bf16[256,512]{1,0:T(8,128)(2,1)S(1)}, bf16[256,512]{1,0:T(8,128)(2,1)}, u32[]{:S(2)}) copy-start(bf16[256,512]{1,0:T(8,128)(2,1)} %param.10) | copy-start | bytes 786436
  228.8 12.6 %copy-start.13 = (s32[64,32]{0,1:T(8,128)S(1)}, s32[64,32]{0,1:T(8,128)}, u32[]{:S(2)}) copy-start(s32[64,32]{0,1:T(8,128)} %param.14) | copy-start | bytes 24580
  228.8 14.4 %copy-start.12 = (s32[64,32]{0,1:T(8,128)S(1)}, s32[64,32]{0,1:T(8,128)}, u32[]{:S(2)}) copy-start(s32[64,32]{0,1:T(8,128)} %param.15) | copy-start | bytes 24580
  228.8 14.6 %copy-start.9 = (bf16[256,512]{1,0:T(8,128)(2,1)S(1)}, bf16[256,512]{1,0:T(8,128)(2,1)}, u32[]{:S(2)}) copy-start(bf16[256,512]{1,0:T(8,128)(2,1)} %param.9) | copy-start | bytes 786436
  228.8 213.6 %all-to-all-start.1 = ((bf16[64,128,512]{2,1,0:T(8,128)(2,1)}), bf16[64,128,512]{2,1,0:T(8,128)(2,1)}, u32[]{:S(2)}, u32[]{:S(2)}) async-start(bf16[64,128,512]{2,1,0:T(8,128)(2,1)} %get-tuple-element.363), calls=%async_computation.1 | async-start | bytes 16777216 | tf_op jit(solution)/shard_map/all_to_all | solution.py:102
  234.9 186.7 %all-gather.2.cloned.1.call-start = ((), (), s32[]{:S(2)}) async-start(), calls=%async_computation.4 | async-start | bytes 1310720 | tf_op jit(solution)/shard_map/all_gather | solution.py:109
  235.7 329.3 %reduce-scatter.5.cloned.1.call-start = ((), (), s32[]{:S(2)}) async-start(), calls=%async_computation.5 | async-start | bytes 1310720 | tf_op jit(solution)/shard_map/reduce_scatter | solution.py:136
  235.7 182.4 %collective-permute-start.1 = (bf16[256,512]{1,0:T(8,128)(2,1)S(1)}, bf16[256,512]{1,0:T(8,128)(2,1)S(1)}, u32[]{:S(2)}, u32[]{:S(2)}) collective-permute-start(bf16[256,512]{1,0:T(8,128)(2,1)S(1)} %copy-done.2), channel_id=1, source_target_pairs={{0,4},{4,8},{8,12},{12,16},{16,20},{20,24},{24,28},{28,32},{32,36}... | collective-permute-start | bytes 786440 | tf_op jit(solution)/shard_map/ppermute | solution.py:15
  239.3 181.6 %collective-permute-start = (bf16[256,512]{1,0:T(8,128)(2,1)S(1)}, bf16[256,512]{1,0:T(8,128)(2,1)S(1)}, u32[]{:S(2)}, u32[]{:S(2)}) collective-permute-start(bf16[256,512]{1,0:T(8,128)(2,1)S(1)} %copy-done.3), channel_id=1, source_target_pairs={{0,4},{4,8},{8,12},{12,16},{16,20},{20,24},{24,28},{28,32},{32,36}... | collective-permute-start | bytes 786440 | tf_op jit(solution)/shard_map/ppermute | solution.py:15
  466.1 5.7 copy-start.1
  469.4 2.5 copy-start.5
  477.7 0.7 copy-start.4
  502.4 5.7 copy-start.1
  505.7 2.5 copy-start.5
  514.1 0.7 copy-start.4
  535.7 2.9 copy-start.6
  538.5 171.4 %reduce-scatter.7.cloned.1.call-start = ((), (), s32[]{:S(2)}) async-start(), calls=%async_computation.6 | async-start | bytes 4259840
  547.6 0.9 copy-start.10
  547.6 6.3 copy-start.8
  547.6 6.6 copy-start.7
  547.6 7.0 copy-start.11
  548.8 8.8 %collective-permute-start.3 = (bf16[256,512]{1,0:T(8,128)(2,1)S(1)}, bf16[256,512]{1,0:T(8,128)(2,1)S(1)}, u32[]{:S(2)}, u32[]{:S(2)}) collective-permute-start(bf16[256,512]{1,0:T(8,128)(2,1)S(1)} %bitcast.279), channel_id=1, source_target_pairs={{4,0},{8,4},{12,8},{16,12},{20,16},{24,20},{28,24},{32,28},{36,32}... | collective-permute-start | bytes 786440 | tf_op jit(solution)/shard_map/ppermute | solution.py:15
  551.9 8.8 %collective-permute-start.2 = (bf16[256,512]{1,0:T(8,128)(2,1)S(1)}, bf16[256,512]{1,0:T(8,128)(2,1)S(1)}, u32[]{:S(2)}, u32[]{:S(2)}) collective-permute-start(bf16[256,512]{1,0:T(8,128)(2,1)S(1)} %bitcast.280), channel_id=1, source_target_pairs={{4,0},{8,4},{12,8},{16,12},{20,16},{24,20},{28,24},{32,28},{36,32}... | collective-permute-start | bytes 786440 | tf_op jit(solution)/shard_map/ppermute | solution.py:15
Sparse Core Ops, SparseCore 0:
  237.6 26.5 all-gather.1
  538.7 26.2 reduce-scatter.4
  570.2 139.6 reduce-scatter.6
where the time goes:
time: 723 us; the launch traced here: 716 us
  waiting for transfers between devices  329 us (46%)
  blocking collectives  199 us (28%)
  matrix products  74.5 us (10%)
  local copies, waits for them, and re-layouts  66 us (9%)
  other arithmetic  17.5 us (2%)
  starting transfers between devices  15.7 us (2%)
  between operations  14 us (2%)
    all_to_all x1, blocking collectives, per_device(): lax.all_to_all(send_k, 'seg', split_axis=0, concat_axis=0, tiled=True)  199 us
    ppermute x4, waiting for transfers between devices, shifted(): return lax.ppermute(block, axis, route)  180 us
    unnamed x4, waiting for transfers between devices  146 us
    dot_general x30, matrix products, product(): jnp.einsum(form, left_side, right_side, preferred_element_type=jnp.float32)  66.1 us
  transfers between devices with their start and end apart: 8, of which 6 were waited for; matrix products, arithmetic and copies ran while one was open for 5% of the time, Pallas kernels for 0%

commit v1 on v0

v1 whole, which is shorter than its diff:
```python
import math

import jax
import jax.numpy as jnp
from jax import lax
from jax.experimental import pallas as pl
from jax.experimental.pallas import tpu as pltpu
from jax.sharding import PartitionSpec as P

DH = 128
BLOCK = 128
SEG = 256
R = 32
NY, NZ, NC, NX = 4, 8, 2, 4
MESH = pl.DeviceIdType.MESH
F32, BF16 = jnp.float32, jnp.bfloat16
NEG = -1e30
SURE = 24
PER = 4
WIDE = PER * BLOCK
CHUNKS = R // PER


def dot_nt(a, b):
    return lax.dot_general(a, b, (((1,), (1,)), ((), ())), preferred_element_type=F32)


def dot_nn(a, b):
    return lax.dot_general(a, b, (((1,), (0,)), ((), ())), preferred_element_type=F32)


def dot_tn(a, b):
    return lax.dot_general(a, b, (((0,), (0,)), ((), ())), preferred_element_type=F32)


def kernel(
    owner_ref, block_ref, q_ref, k_ref, v_ref, g_ref, w_ref,
    lo_ref, dq_ref, dk_ref, dv_ref, pg_ref,
    kv, q4, do4, dal, fg, s_mem, s_near, p_mem, stat, attn4, attn_in, lo_out, lo_in,
    pp, rs0, r1, rs1, r2, rs2, dq_acc, near_acc, carry_out, carry_in, gq, gk, gv,
    loc, ys, yr, xs, xr, zs, zr, ms, mr, ds_, dr, as_, ar, cs, cr, bs, br, rys, ryr, rzs, rzr, ls, lr, os_, or_,
):
    s_me = lax.axis_index("seg")
    x = lax.axis_index("head")
    c = lax.rem(s_me, NC)
    z = lax.rem(lax.div(s_me, NC), NZ)
    y = lax.div(s_me, NC * NZ)
    scale = 1.0 / math.sqrt(DH)
    scale2 = scale * math.log2(math.e)

    def seg_of(yy, zz, cc):
        return (yy * NZ + zz) * NC + cc

    y_of = [lax.rem(y + d, NY) for d in range(NY)]
    x_of = [lax.rem(x + d, NX) for d in range(NX)]
    z_of = [lax.rem(z + d, NZ) for d in range(NZ)]
    y_peer = [(seg_of(y_of[d], z, c), x) for d in range(NY)]
    z_peer = [(seg_of(y, z_of[d], c), x) for d in range(NZ)]
    x_peer = [(s_me, x_of[d]) for d in range(NX)]
    sibling = (seg_of(y, z, 1 - c), x)
    cross = (seg_of(y, lax.rem(z + NZ - 1 + 2 * c, NZ), 1 - c), x)
    back = (seg_of(y, lax.rem(z + NZ - 1 + c, NZ), 1 - c), x)
    wrap = 1 - jnp.minimum(z + c, 1)

    sends = []

    def send(src, dst, ssem, rsem, dev):
        copy = pltpu.make_async_remote_copy(
            src_ref=src, dst_ref=dst, send_sem=ssem, recv_sem=rsem, device_id=dev, device_id_type=MESH
        )
        copy.start()
        sends.append(copy)

    def arrived(dst, ssem, rsem):
        pltpu.make_async_remote_copy(
            src_ref=dst, dst_ref=dst, send_sem=ssem, recv_sem=rsem, device_id=sibling, device_id_type=MESH
        ).wait_recv()

    def cols(i):
        return pl.ds(pl.multiple_of(i * DH, DH), DH)

    def slot(plane, rz, ry):
        return (plane * NZ + rz) * NY + ry

    own = [
        pltpu.make_async_copy(k_ref.at[:, :, cols(y)], kv.at[0, 0], loc.at[0]),
        pltpu.make_async_copy(v_ref.at[:, :, cols(y)], kv.at[0, 1], loc.at[1]),
        pltpu.make_async_copy(q_ref.at[:, cols(y)], q4.at[0], loc.at[2]),
        pltpu.make_async_copy(g_ref, fg.at[x], loc.at[3]),
    ]
    for copy in own:
        copy.start()

    barrier = pltpu.get_barrier_semaphore()
    peers = y_peer[1:] + z_peer[1:] + x_peer[1:] + [sibling, cross]
    for dev in peers:
        pl.semaphore_signal(barrier, inc=1, device_id=dev, device_id_type=MESH)
    pl.semaphore_wait(barrier, len(peers))

    for d in (1, 3, 2):
        send(k_ref.at[:, :, cols(y_of[d])], kv.at[NY - d, 0], ys.at[d - 1, 0], yr.at[NY - d - 1, 0], y_peer[d])
        send(v_ref.at[:, :, cols(y_of[d])], kv.at[NY - d, 1], ys.at[d - 1, 1], yr.at[NY - d - 1, 1], y_peer[d])
    for d in (1, 3, 2):
        send(g_ref, fg.at[x], xs.at[d - 1], xr.at[d - 1], x_peer[d])
    for copy in own:
        copy.wait()
    order = (0, 1, 3, 2)

    def z_step(t):
        up, down = (NZ - t) % NZ, t
        for ry in order:
            if t == 0:
                if ry:
                    arrived(kv.at[ry, 0], ys.at[ry - 1, 0], yr.at[ry - 1, 0])
                    arrived(kv.at[ry, 1], ys.at[ry - 1, 1], yr.at[ry - 1, 1])
            else:
                arrived(kv.at[slot(0, up, ry)], zs.at[0, t - 1, ry], zr.at[0, t - 1, ry])
                arrived(kv.at[slot(0, down, ry)], zs.at[1, t - 1, ry], zr.at[1, t - 1, ry])
            if t < NZ // 2 - 1:
                send(kv.at[slot(0, up, ry)], kv.at[slot(0, NZ - 1 - t, ry)], zs.at[0, t, ry], zr.at[0, t, ry], z_peer[1])
                send(kv.at[slot(0, down, ry)], kv.at[slot(0, t + 1, ry)], zs.at[1, t, ry], zr.at[1, t, ry], z_peer[NZ - 1])
            else:
                far = slot(0, NZ // 2, ry)
                send(kv.at[slot(0, up, ry), 0], kv.at[far, 0], zs.at[0, t, ry], zr.at[0, t, ry], z_peer[1])
                send(kv.at[slot(0, down, ry), 1], kv.at[far, 1], zs.at[1, t, ry], zr.at[1, t, ry], z_peer[NZ - 1])
            for rz in ((0,) if t == 0 else (up, down)):
                send(kv.at[slot(0, rz, ry)], kv.at[slot(1, rz, ry)], ms.at[rz, ry], mr.at[rz, ry], sibling)

    z_step(0)
    for d in (1, 3, 2):
        send(q_ref.at[:, cols(y_of[d])], q4.at[NY - d], ys.at[d - 1, 2], yr.at[NY - d - 1, 2], y_peer[d])

    for d in (1, 3, 2):
        arrived(fg.at[x_of[NX - d]], xs.at[d - 1], xr.at[d - 1])
    width = g_ref.shape[1]
    da = dot_nt(fg[0], w_ref[:, :width])
    for i in range(1, NX):
        da += dot_nt(fg[i], w_ref[:, i * width : (i + 1) * width])
    da = da.astype(BF16)
    for i in range(NY):
        dal[i] = da[:, i * DH : (i + 1) * DH]
    do4[0] = dal[y]
    for d in (1, 3, 2):
        send(dal.at[y_of[d]], do4.at[NY - d], ds_.at[d - 1], dr.at[NY - d - 1], y_peer[d])

    for t in range(1, NZ // 2):
        z_step(t)
    for ry in order:
        far = slot(0, NZ // 2, ry)
        t = NZ // 2 - 1
        arrived(kv.at[far, 0], zs.at[0, t, ry], zr.at[0, t, ry])
        arrived(kv.at[far, 1], zs.at[1, t, ry], zr.at[1, t, ry])
        send(kv.at[far], kv.at[slot(1, NZ // 2, ry)], ms.at[NZ // 2, ry], mr.at[NZ // 2, ry], sibling)
    for ry in range(1, NY):
        arrived(q4.at[ry], ys.at[ry - 1, 2], yr.at[ry - 1, 2])
        arrived(do4.at[ry], ds_.at[ry - 1], dr.at[ry - 1])
    for rz in range(NZ):
        for ry in range(NY):
            arrived(kv.at[slot(1, rz, ry)], ms.at[rz, ry], mr.at[rz, ry])

    causal = lax.broadcasted_iota(jnp.int32, (SEG, SEG), 0) >= lax.broadcasted_iota(jnp.int32, (SEG, SEG), 1)

    def seg_id(ry):
        return seg_of(lax.rem(y + ry, NY), z, c)

    def cache_slot(ry):
        return slot(1, (NZ - 1) * (1 - c), lax.rem(ry + NY - wrap, NY))

    def place(ry, j):
        o = owner_ref[seg_id(ry), j]
        b = jnp.maximum(block_ref[seg_id(ry), j], 0)
        oc = lax.rem(o, NC)
        oz = lax.rem(lax.div(o, NC), NZ)
        oy = lax.div(o, NC * NZ)
        plane = lax.rem(oc + c, NC)
        rz = lax.rem(oz + NZ - z, NZ)
        return slot(plane, rz, lax.rem(oy + NY - y, NY)), b

    def stored(ry, i, which):
        parts = []
        for b in range(PER):
            at, half = place(ry, i * PER + b)
            parts.append(kv[at, which, half])
        return jnp.concatenate(parts, axis=0)

    def near(ref_at, which):
        return kv[ref_at, which].reshape(SEG, DH)

    def fold(m, entry, op):
        for i in range(entry.shape[1] // DH):
            m = op(m, entry[:, i * DH : (i + 1) * DH])
        return m

    def forward(ry):
        q = q4[ry]
        s_own = jnp.where(causal, dot_nt(q, near(ry, 0)), NEG)
        s_near[ry, 0] = s_own
        top = fold(s_own[:, :DH], s_own[:, DH:], jnp.maximum)
        has_cache = jnp.minimum(seg_id(ry), 1).astype(F32)
        s_cache = dot_nt(q, near(cache_slot(ry), 0)) + (1.0 - has_cache) * NEG
        s_near[ry, 1] = s_cache
        top = fold(top, s_cache, jnp.maximum)

        def score(i, top, sure):
            s = dot_nt(q, stored(ry, i, 0))
            if not sure:
                parts = []
                for b in range(PER):
                    dead = jnp.maximum(-block_ref[seg_id(ry), i * PER + b], 0).astype(F32)
                    parts.append(s[:, b * BLOCK : (b + 1) * BLOCK] + dead * NEG)
                s = jnp.concatenate(parts, axis=1)
            s_mem[i] = s
            return fold(top, s, jnp.maximum)

        top = lax.fori_loop(0, SURE // PER, lambda i, m: score(i, m, True), top)
        top = lax.fori_loop(SURE // PER, CHUNKS, lambda i, m: score(i, m, False), top)
        top = jnp.max(top, axis=1, keepdims=True)
        total = jnp.zeros((SEG, DH), F32)
        mixed = jnp.zeros((SEG, DH), F32)
        for part, at in ((0, ry), (1, cache_slot(ry))):
            p = jnp.exp2((s_near[ry, part] - top) * scale2)
            total = fold(total, p, jnp.add)
            mixed += dot_nn(p.astype(BF16), near(at, 1))

        def mix(i, held):
            total, mixed = held
            p = jnp.exp2((s_mem[i] - top) * scale2)
            total = fold(total, p, jnp.add)
            p = p.astype(BF16)
            p_mem[ry, i] = p
            return total, mixed + dot_nn(p, stored(ry, i, 1))

        total, mixed = lax.fori_loop(0, CHUNKS, mix, (total, mixed))
        inv = 1.0 / jnp.sum(total, axis=1, keepdims=True)
        attn = (mixed * inv).astype(BF16)
        attn4[ry] = attn
        delta = jnp.sum(do4[ry].astype(F32) * attn.astype(F32), axis=1, keepdims=True)
        stat[ry, 0] = jnp.broadcast_to(top, (SEG, DH))
        stat[ry, 1] = jnp.broadcast_to(inv, (SEG, DH))
        stat[ry, 2] = jnp.broadcast_to(delta, (SEG, DH))

    def backward_near(ry):
        q, do = q4[ry], do4[ry]
        top, inv, delta = stat[ry, 0, :, :1], stat[ry, 1, :, :1], stat[ry, 2, :, :1]
        dq = jnp.zeros((SEG, DH), F32)
        for part, at in ((0, ry), (1, cache_slot(ry))):
            weights = jnp.exp2((s_near[ry, part] - top) * scale2) * inv
            slopes = (weights * (dot_nt(do, near(at, 1)) - delta)).astype(BF16)
            dq += dot_nn(slopes, near(at, 0))
            gk_part = dot_tn(slopes, q) * scale
            gv_part = dot_tn(weights.astype(BF16), do)
            if part == 0:
                near_acc[ry, 0] = gk_part
                near_acc[ry, 1] = gv_part
            else:
                carry_out[ry, 0] = gk_part.astype(BF16)
                carry_out[ry, 1] = gv_part.astype(BF16)
        dq_acc[ry] = dq

    def backward_mem(ry):
        do = do4[ry]
        inv, delta = stat[ry, 1, :, :1], stat[ry, 2, :, :1]

        def step(i, dq):
            slopes = (p_mem[ry, i].astype(F32) * (dot_nt(do, stored(ry, i, 1)) - delta)).astype(BF16)
            return dq + dot_nn(slopes, stored(ry, i, 0))

        dq = lax.fori_loop(0, CHUNKS, step, jnp.zeros((SEG, DH), F32))
        gq[ry] = ((dq_acc[ry] + dq * inv) * scale).astype(BF16)

    for ry in range(NY):
        forward(ry)
        if ry:
            send(attn4.at[ry], attn_in.at[y], as_.at[ry - 1], ar.at[ry - 1], y_peer[ry])
    attn_in[y] = attn4[0]

    for ry in range(NY):
        backward_near(ry)
        to = lax.rem(ry + NY - wrap, NY)
        send(carry_out.at[ry], carry_in.at[to], cs.at[ry], cr.at[to], back)

    for d in range(1, NY):
        arrived(attn_in.at[y_of[NY - d]], as_.at[d - 1], ar.at[d - 1])
    attn = jnp.concatenate([attn_in[i] for i in range(NY)], axis=1)
    wide = attn.shape[1]
    rows = pg_ref.shape[0]
    for i in range(NY):
        part = dot_tn(fg[i], attn).reshape(NZ, NC, rows, wide)
        pp[i] = part.astype(BF16)
        send(pp.at[i, :, 1 - c], rs0.at[i], bs.at[i], br.at[i], sibling)
    for i in range(NX):
        lo_out[i] = dot_nn(attn, w_ref[:, i * width : (i + 1) * width]).astype(BF16)
    for d in (1, 3, 2):
        send(lo_out.at[x_of[d]], lo_in.at[d - 1], ls.at[d - 1], lr.at[d - 1], x_peer[d])

    backward_mem(0)
    for i in range(NY):
        arrived(rs0.at[i], bs.at[i], br.at[i])
        r1[i] = (pp[i, :, c].astype(F32) + rs0[i].astype(F32)).astype(BF16)
    for d in (1, 3, 2):
        send(r1.at[y_of[d]], rs1.at[d - 1], rys.at[d - 1], ryr.at[d - 1], y_peer[d])
    backward_mem(1)
    send(gq.at[1], dq_ref.at[:, cols(y)], os_.at[0, 0], or_.at[0, 0], y_peer[1])
    for ry in range(NY):
        arrived(carry_in.at[ry], cs.at[ry], cr.at[ry])
        gk[ry] = (near_acc[ry, 0] + carry_in[ry, 0].astype(F32)).astype(BF16)
        gv[ry] = (near_acc[ry, 1] + carry_in[ry, 1].astype(F32)).astype(BF16)
        if ry:
            send(gk.at[ry], dk_ref.at[:, cols(y)], os_.at[1, ry - 1], or_.at[1, ry - 1], y_peer[ry])
            send(gv.at[ry], dv_ref.at[:, cols(y)], os_.at[2, ry - 1], or_.at[2, ry - 1], y_peer[ry])
    backward_mem(2)
    send(gq.at[2], dq_ref.at[:, cols(y)], os_.at[0, 1], or_.at[0, 1], y_peer[2])
    total = r1[y].astype(F32)
    for d in range(1, NY):
        arrived(rs1.at[d - 1], rys.at[d - 1], ryr.at[d - 1])
        total += rs1[d - 1].astype(F32)
    r2[...] = total.astype(BF16)
    for d in range(1, NZ):
        send(r2.at[z_of[d]], rs2.at[d - 1], rzs.at[d - 1], rzr.at[d - 1], z_peer[d])
    backward_mem(3)
    send(gq.at[3], dq_ref.at[:, cols(y)], os_.at[0, 2], or_.at[0, 2], y_peer[3])

    home = [
        pltpu.make_async_copy(gq.at[0], dq_ref.at[:, cols(y)], loc.at[0]),
        pltpu.make_async_copy(gk.at[0], dk_ref.at[:, cols(y)], loc.at[1]),
        pltpu.make_async_copy(gv.at[0], dv_ref.at[:, cols(y)], loc.at[2]),
    ]
    for copy in home:
        copy.start()
    out = lo_out[x].astype(F32)
    for d in range(1, NX):
        arrived(lo_in.at[d - 1], ls.at[d - 1], lr.at[d - 1])
        out += lo_in[d - 1].astype(F32)
    lo_ref[...] = out.astype(BF16)
    total = r2[z].astype(F32)
    for d in range(1, NZ):
        arrived(rs2.at[d - 1], rzs.at[d - 1], rzr.at[d - 1])
        total += rs2[d - 1].astype(F32)
    pg_ref[...] = total
    for n, ref in enumerate((dq_ref, dk_ref, dv_ref)):
        for d in range(1, NY):
            arrived(ref.at[:, cols(y_of[NY - d])], os_.at[n, d - 1], or_.at[n, d - 1])
    for copy in home:
        copy.wait()
    for copy in sends:
        copy.wait_send()


def per_device(queries, keys, values, out_grad, out_weight, retr_owner, retr_block):
    tok, wide = queries.shape
    full = out_weight.shape[1]
    rows = full // (NY * NZ * NC)
    vmem = pl.BlockSpec(memory_space=pltpu.VMEM)
    smem = pl.BlockSpec(memory_space=pltpu.SMEM)
    dma = pltpu.SemaphoreType.DMA
    tile = (tok, DH)
    halves = tok // BLOCK
    scratch = [
        pltpu.VMEM((NC * NZ * NY, 2, halves, BLOCK, DH), BF16),
        pltpu.VMEM((NY,) + tile, BF16),
        pltpu.VMEM((NY,) + tile, BF16),
        pltpu.VMEM((NY,) + tile, BF16),
        pltpu.VMEM((NX, tok, wide), BF16),
        pltpu.VMEM((CHUNKS, tok, WIDE), F32),
        pltpu.VMEM((NY, 2, tok, tok), F32),
        pltpu.VMEM((NY, CHUNKS, tok, WIDE), BF16),
        pltpu.VMEM((NY, 3) + tile, F32),
        pltpu.VMEM((NY,) + tile, BF16),
        pltpu.VMEM((NY,) + tile, BF16),
        pltpu.VMEM((NX, tok, wide), BF16),
        pltpu.VMEM((NX - 1, tok, wide), BF16),
        pltpu.VMEM((NY, NZ, NC, rows, wide), BF16),
        pltpu.VMEM((NY, NZ, rows, wide), BF16),
        pltpu.VMEM((NY, NZ, rows, wide), BF16),
        pltpu.VMEM((NY - 1, NZ, rows, wide), BF16),
        pltpu.VMEM((NZ, rows, wide), BF16),
        pltpu.VMEM((NZ - 1, rows, wide), BF16),
        pltpu.VMEM((NY,) + tile, F32),
        pltpu.VMEM((NY, 2) + tile, F32),
        pltpu.VMEM((NY, 2) + tile, BF16),
        pltpu.VMEM((NY, 2) + tile, BF16),
        pltpu.VMEM((NY,) + tile, BF16),
        pltpu.VMEM((NY,) + tile, BF16),
        pltpu.VMEM((NY,) + tile, BF16),
        dma((4,)),
        dma((NY - 1, 3)), dma((NY - 1, 3)),
        dma((NX - 1,)), dma((NX - 1,)),
        dma((2, NZ // 2, NY)), dma((2, NZ // 2, NY)),
        dma((NZ, NY)), dma((NZ, NY)),
        dma((NY - 1,)), dma((NY - 1,)),
        dma((NY - 1,)), dma((NY - 1,)),
        dma((NY,)), dma((NY,)),
        dma((NY,)), dma((NY,)),
        dma((NY - 1,)), dma((NY - 1,)),
        dma((NZ - 1,)), dma((NZ - 1,)),
        dma((NX - 1,)), dma((NX - 1,)),
        dma((3, NY - 1)), dma((3, NY - 1)),
    ]
    grad = jax.ShapeDtypeStruct((tok, wide), BF16)
    return pl.pallas_call(
        kernel,
        out_shape=(grad, grad, grad, grad, jax.ShapeDtypeStruct((rows, wide), F32)),
        in_specs=[smem, smem] + [vmem] * 5,
        out_specs=(vmem,) * 5,
        scratch_shapes=scratch,
        compiler_params=pltpu.CompilerParams(
            collective_id=0, has_side_effects=True, vmem_limit_bytes=60 * 1024 * 1024
        ),
    )(
        retr_owner,
        retr_block,
        queries,
        keys.reshape(halves, BLOCK, wide),
        values.reshape(halves, BLOCK, wide),
        out_grad,
        out_weight,
    )


def solution(mesh):
    rows = P("seg", "head")
    return jax.shard_map(
        per_device,
        mesh=mesh,
        in_specs=(rows, rows, rows, rows, P("head", None), P(), P()),
        out_specs=(rows,) * 5,
        check_vma=False,
    )
```

time: 723 us -> 124 us (0.17)
  waiting for transfers between devices: 329 us -> 0 us
  blocking collectives: 199 us -> 0 us
  Pallas kernels: 0 us -> 113 us
  matrix products: 74.5 us -> 0 us
  local copies, waits for them, and re-layouts: 66 us -> 10.2 us
  other arithmetic: 17.5 us -> 0 us
  starting transfers between devices: 15.7 us -> 0 us
  between operations: 14 us -> 0.65 us
    all_to_all x1 -> x0, blocking collectives: 199 us -> none  [per_device(): lax.all_to_all(send_k, 'seg', split_axis=0, concat_axis=0, tiled=True)]
    ppermute x4 -> x0, waiting for transfers between devices: 180 us -> none  [shifted(): return lax.ppermute(block, axis, route)]
    unnamed x4 -> x0, waiting for transfers between devices: 146 us -> none
    pallas_call x0 -> x1, Pallas kernels: none -> 113 us  [per_device(): pl.pallas_call(kernel, out_shape=(grad, grad, grad, grad, jax.ShapeDtypeS...]
    dot_general x33 -> x0, matrix products: 74.5 us -> none  [the longest x30 66.1 us: product(): jnp.einsum(form, left_side, right_side, preferred_element_type=jnp.float32)]
    gather x4 -> x0, local copies, waits for them, and re-layouts: 24 us -> none  [the longest x1 6.31 us: per_device(): send_k = jnp.where(served, key_blocks[wanted], zero_fill)]
    another operation x2 -> x0, local copies, waits for them, and re-layouts: 13.8 us -> none  [split_heads(): return tok_rows.reshape(tok_rows.shape[0], count, -1).transpose(1, 0, 2)]
    ppermute x4 -> x0, starting transfers between devices: 9.44 us -> none  [shifted(): return lax.ppermute(block, axis, route)]
  transfers between devices with their start and end apart: 8 -> 0, of which waited for: 6 -> 0; matrix products, arithmetic and copies ran while one was open for 5% -> 0% of each run, Pallas kernels for 0% -> 0%
where the time goes in v1:
time: 124 us
  Pallas kernels  113 us (91%)
  local copies, waits for them, and re-layouts  10.2 us (8%)
    pallas_call x1, Pallas kernels, per_device(): pl.pallas_call(kernel, out_shape=(grad, grad, grad, grad, jax.ShapeDtypeS...  113 us
    unnamed x9, local copies, waits for them, and re-layouts  10.2 us

profile of v1, /device:TPU:1, one launch (start us, length us, event | category | flops | bytes accessed | tf_op | source)
XLA Modules:
  0.0 124.1 jit_solution(1074826699002659300)
XLA Ops:
  0.6 1.4 %copy.12.owner_ref = s32[64,32]{1,0:T(8,128)} copy(s32[64,32]{0,1:T(8,128)} %param.12) | data formatting | bytes 16384 | tf_op args[5]
  2.0 1.4 %copy.13.block_ref = s32[64,32]{1,0:T(8,128)} copy(s32[64,32]{0,1:T(8,128)} %param.13) | data formatting | bytes 16384 | tf_op args[6]
  3.5 113.2 %shard_map.110 = (bf16[256,512]{1,0:T(8,128)(2,1)}, bf16[256,512]{1,0:T(8,128)(2,1)}, bf16[256,512]{1,0:T(8,128)(2,1)}, bf16[256,512]{1,0:T(8,128)(2,1)}, f32[32,512]{1,0:T(8,128)}) custom-call(s32[64,32]{1,0:T(8,128)} %copy.12.owner_ref, s32[64,32]{1,0:T(8,128)} %copy.13.block_ref, bf16[256,512]{1,0:T(8,128)(2,1)} %q_ref.1, bf16[2,128,512]{2,1,0:T(8,128)(2,1)} %bitcast.2, ...), custom_call_target="tpu_custom_call" | custom-call | tf_op jit(solution)/shard_map/pallas_call | solution.py:400
  116.7 0.0 copy-start
  116.7 1.7 %copy.19 = bf16[256,512]{1,0:T(8,128)(2,1)} copy(bf16[256,512]{1,0:T(8,128)(2,1)} %get-tuple-element.10) | data formatting | bytes 524288
  118.4 1.7 %copy.20 = bf16[256,512]{1,0:T(8,128)(2,1)} copy(bf16[256,512]{1,0:T(8,128)(2,1)} %get-tuple-element.11) | data formatting | bytes 524288
  120.1 1.7 %copy.21 = bf16[256,512]{1,0:T(8,128)(2,1)} copy(bf16[256,512]{1,0:T(8,128)(2,1)} %get-tuple-element.12) | data formatting | bytes 524288
  121.8 1.7 %copy.22 = bf16[256,512]{1,0:T(8,128)(2,1)} copy(bf16[256,512]{1,0:T(8,128)(2,1)} %get-tuple-element.13) | data formatting | bytes 524288
  123.4 0.0 copy-done
  123.4 0.6 copy.23
Async XLA Ops:
  116.7 6.7 %copy-start = (f32[32,512]{1,0:T(8,128)S(1)}, f32[32,512]{1,0:T(8,128)}, u32[]{:S(2)}) copy-start(f32[32,512]{1,0:T(8,128)} %get-tuple-element.14) | copy-start | bytes 196612

commit v2 on v1

v2 whole, which is shorter than its diff:
```python
import math

import jax
import jax.numpy as jnp
from jax import lax
from jax.experimental import pallas as pl
from jax.experimental.pallas import tpu as pltpu
from jax.sharding import PartitionSpec as P

DH = 128
BLOCK = 128
SEG = 256
R = 32
NY, NZ, NC, NX = 4, 8, 2, 4
MESH = pl.DeviceIdType.MESH
F32, BF16 = jnp.float32, jnp.bfloat16
NEG = -1e30
SURE = 24
PER = 4
WIDE = PER * BLOCK
CHUNKS = R // PER


def dot_nt(a, b):
    return lax.dot_general(a, b, (((1,), (1,)), ((), ())), preferred_element_type=F32)


def dot_nn(a, b):
    return lax.dot_general(a, b, (((1,), (0,)), ((), ())), preferred_element_type=F32)


def dot_tn(a, b):
    return lax.dot_general(a, b, (((0,), (0,)), ((), ())), preferred_element_type=F32)


def kernel(
    owner_ref, block_ref, q_ref, k_ref, v_ref, g_ref, w_ref,
    lo_ref, dq_ref, dk_ref, dv_ref, pg_ref,
    kv, kvc, q4, do4, dal, fg, fgt, s_near, p_mem, m_mem, top4, sum4, mix4, stat, attn4, attn_in, lo_out, lo_in,
    pp, rs0, r1, ra, rb, ra_out, rb_out, ra2, rb2, r2, rs2, dq_acc, near_acc, carry_out, carry_in, gq, gk, gv,
    tab_v, tab,
    loc, ys, yr, xs, xr, zs, zr, ms, mr, ds_, dr, as_, ar, cs, cr, bs, br, rys, ryr, rzs, rzr, ls, lr, os_, or_,
):
    s_me = lax.axis_index("seg")
    x = lax.axis_index("head")
    c = lax.rem(s_me, NC)
    z = lax.rem(lax.div(s_me, NC), NZ)
    y = lax.div(s_me, NC * NZ)
    scale = 1.0 / math.sqrt(DH)
    scale2 = scale * math.log2(math.e)

    def seg_of(yy, zz, cc):
        return (yy * NZ + zz) * NC + cc

    y_of = [lax.rem(y + d, NY) for d in range(NY)]
    x_of = [lax.rem(x + d, NX) for d in range(NX)]
    z_of = [lax.rem(z + d, NZ) for d in range(NZ)]
    y_peer = [(seg_of(y_of[d], z, c), x) for d in range(NY)]
    z_peer = [(seg_of(y, z_of[d], c), x) for d in range(NZ)]
    x_peer = [(s_me, x_of[d]) for d in range(NX)]
    sibling = (seg_of(y, z, 1 - c), x)
    cross = (seg_of(y, lax.rem(z + NZ - 1 + 2 * c, NZ), 1 - c), x)
    back = (seg_of(y, lax.rem(z + NZ - 1 + c, NZ), 1 - c), x)
    wrap = 1 - jnp.minimum(z + c, 1)

    sends = []

    def send(src, dst, ssem, rsem, dev):
        copy = pltpu.make_async_remote_copy(
            src_ref=src, dst_ref=dst, send_sem=ssem, recv_sem=rsem, device_id=dev, device_id_type=MESH
        )
        copy.start()
        sends.append(copy)

    def arrived(dst, ssem, rsem):
        pltpu.make_async_remote_copy(
            src_ref=dst, dst_ref=dst, send_sem=ssem, recv_sem=rsem, device_id=sibling, device_id_type=MESH
        ).wait_recv()

    def cols(i):
        return pl.ds(pl.multiple_of(i * DH, DH), DH)

    def slot(plane, rz, ry):
        return (plane * NZ + rz) * NY + ry

    own = [
        pltpu.make_async_copy(k_ref.at[:, :, cols(y)], kv.at[0, 0], loc.at[0]),
        pltpu.make_async_copy(v_ref.at[:, :, cols(y)], kv.at[0, 1], loc.at[1]),
        pltpu.make_async_copy(q_ref.at[:, cols(y)], q4.at[0], loc.at[2]),
        pltpu.make_async_copy(g_ref, fg.at[x], loc.at[3]),
    ]
    for copy in own:
        copy.start()

    barrier = pltpu.get_barrier_semaphore()
    peers = y_peer[1:] + z_peer[1:] + x_peer[1:] + [sibling, cross]
    for dev in peers:
        pl.semaphore_signal(barrier, inc=1, device_id=dev, device_id_type=MESH)
    pl.semaphore_wait(barrier, len(peers))

    for d in (1, 3, 2):
        send(k_ref.at[:, :, cols(y_of[d])], kv.at[NY - d, 0], ys.at[d - 1, 0], yr.at[NY - d - 1, 0], y_peer[d])
        send(v_ref.at[:, :, cols(y_of[d])], kv.at[NY - d, 1], ys.at[d - 1, 1], yr.at[NY - d - 1, 1], y_peer[d])
    send(g_ref, fg.at[x], xs.at[0], xr.at[0], x_peer[1])
    send(g_ref, fg.at[x], xs.at[1], xr.at[1], x_peer[NX - 1])
    for copy in own:
        copy.wait()
    order = (0, 1, 3, 2)

    def z_part(t, ry):
        up, down = (NZ - t) % NZ, t
        if t == 0:
            if ry:
                arrived(kv.at[ry, 0], ys.at[ry - 1, 0], yr.at[ry - 1, 0])
                arrived(kv.at[ry, 1], ys.at[ry - 1, 1], yr.at[ry - 1, 1])
        else:
            arrived(kv.at[slot(0, up, ry)], zs.at[0, t - 1, ry], zr.at[0, t - 1, ry])
            arrived(kv.at[slot(0, down, ry)], zs.at[1, t - 1, ry], zr.at[1, t - 1, ry])
        if t < NZ // 2 - 1:
            send(kv.at[slot(0, up, ry)], kv.at[slot(0, NZ - 1 - t, ry)], zs.at[0, t, ry], zr.at[0, t, ry], z_peer[1])
            send(kv.at[slot(0, down, ry)], kv.at[slot(0, t + 1, ry)], zs.at[1, t, ry], zr.at[1, t, ry], z_peer[NZ - 1])
        else:
            far = slot(0, NZ // 2, ry)
            send(kv.at[slot(0, up, ry), 0], kv.at[far, 0], zs.at[0, t, ry], zr.at[0, t, ry], z_peer[1])
            send(kv.at[slot(0, down, ry), 1], kv.at[far, 1], zs.at[1, t, ry], zr.at[1, t, ry], z_peer[NZ - 1])
        for rz in ((0,) if t == 0 else (up, down)):
            send(kv.at[slot(0, rz, ry)], kv.at[slot(1, rz, ry)], ms.at[rz, ry], mr.at[rz, ry], sibling)

    def z_far(ry):
        far, t = slot(0, NZ // 2, ry), NZ // 2 - 1
        arrived(kv.at[far, 0], zs.at[0, t, ry], zr.at[0, t, ry])
        arrived(kv.at[far, 1], zs.at[1, t, ry], zr.at[1, t, ry])
        send(kv.at[far], kv.at[slot(1, NZ // 2, ry)], ms.at[NZ // 2, ry], mr.at[NZ // 2, ry], sibling)

    def take(rz, ry):
        arrived(kv.at[slot(1, rz, ry)], ms.at[rz, ry], mr.at[rz, ry])
        for plane in range(NC):
            kvc[slot(plane, rz, ry)] = kv[slot(plane, rz, ry)]

    def seg_id(ry):
        return seg_of(lax.rem(y + ry, NY), z, c)

    def cache_slot(ry):
        return slot(1, (NZ - 1) * (1 - c), lax.rem(ry + NY - wrap, NY))

    def near(at, which):
        return kvc[at, which].reshape(SEG, DH)

    def fold(m, entry, op):
        for i in range(entry.shape[1] // DH):
            m = op(m, entry[:, i * DH : (i + 1) * DH])
        return m

    def make_table(ry):
        lane = lax.broadcasted_iota(jnp.int32, owner_ref.shape, 1) == seg_id(ry)
        o = jnp.sum(jnp.where(lane, owner_ref[...], 0), axis=1, keepdims=True)
        b = jnp.sum(jnp.where(lane, block_ref[...], 0), axis=1, keepdims=True)
        rz = ((o >> 1) & (NZ - 1)) + NZ - z & (NZ - 1)
        rr = (o >> 4) + NY - y & (NY - 1)
        plane = (o + c) & (NC - 1)
        away = jnp.minimum(rz, NZ - rz)
        dead = b < 0
        turn = rr ^ (rr >> 1)
        stage = jnp.where(away < 3, 0, jnp.where(away == 3, 1 + turn, 1 + NY + turn))
        stage = jnp.where(dead, -1, stage)
        code = jnp.where(dead, 256, ((plane * NZ + rz) * NY + rr) * 2 + jnp.maximum(b, 0))
        down = lax.broadcasted_iota(jnp.int32, (R, R), 0)
        across = lax.broadcasted_iota(jnp.int32, (R, R), 1)
        stage_col = jnp.broadcast_to(stage, (R, R))
        stage_row = jnp.sum(jnp.where(down == across, stage_col, 0), axis=0, keepdims=True)
        first = (stage_row < stage_col) | ((stage_row == stage_col) & (across < down))
        rank = jnp.sum(first.astype(jnp.int32), axis=1, keepdims=True)
        tab_v[ry : ry + 1, :R] = jnp.sum(jnp.where(rank == across, code, 0), axis=0, keepdims=True)

    def stored(ry, i, which):
        parts = []
        for b in range(PER):
            code = tab[ry, i * PER + b]
            parts.append(kvc[(code & 255) >> 1, which, code & 1])
        return jnp.concatenate(parts, axis=0)

    causal = lax.broadcasted_iota(jnp.int32, (SEG, SEG), 0) >= lax.broadcasted_iota(jnp.int32, (SEG, SEG), 1)

    def forward_near(ry):
        q = q4[ry]
        s_own = jnp.where(causal, dot_nt(q, near(ry, 0)), NEG)
        s_near[ry, 0] = s_own
        dead = (1 - jnp.minimum(seg_id(ry), 1)).astype(F32)
        s_cache = dot_nt(q, near(cache_slot(ry), 0)) + dead * NEG
        s_near[ry, 1] = s_cache
        top = fold(fold(s_own[:, :DH], s_own[:, DH:], jnp.maximum), s_cache, jnp.maximum)
        top = jnp.broadcast_to(jnp.max(top, axis=1, keepdims=True), (SEG, DH))
        total = jnp.zeros((SEG, DH), F32)
        mixed = jnp.zeros((SEG, DH), F32)
        wide_top = jnp.concatenate([top] * (SEG // DH), axis=1)
        for s, at in ((s_own, ry), (s_cache, cache_slot(ry))):
            p = jnp.exp2((s - wide_top) * scale2)
            total = fold(total, p, jnp.add)
            mixed += dot_nn(p.astype(BF16), near(at, 1))
        top4[ry], sum4[ry], mix4[ry] = top, total, mixed

    def forward_mem(i):
        def pair(n, _):
            rys = [n * 2, n * 2 + 1]
            scores = [dot_nt(q4[ry], stored(ry, i, 0)) for ry in rys]
            for ry, s in zip(rys, scores):
                if i * PER < R - SURE:
                    parts = []
                    for b in range(PER):
                        dead = (tab[ry, i * PER + b] >> 8).astype(F32)
                        parts.append(s[:, b * BLOCK : (b + 1) * BLOCK] + dead * NEG)
                    s = jnp.concatenate(parts, axis=1)
                old = top4[ry]
                top = jnp.max(fold(s[:, :DH], s[:, DH:], jnp.maximum), axis=1, keepdims=True)
                top = jnp.maximum(old, jnp.broadcast_to(top, (SEG, DH)))
                less = jnp.exp2((old - top) * scale2)
                p = jnp.exp2((s - jnp.concatenate([top] * (WIDE // DH), axis=1)) * scale2)
                sum4[ry] = fold(sum4[ry] * less, p, jnp.add)
                p = p.astype(BF16)
                p_mem[ry, i] = p
                mix4[ry] = mix4[ry] * less + dot_nn(p, stored(ry, i, 1))
                top4[ry] = top
                m_mem[ry, i] = top
            return _

        lax.fori_loop(0, NY // 2, pair, 0)

    def finish(ry):
        inv = 1.0 / jnp.sum(sum4[ry], axis=1, keepdims=True)
        attn = (mix4[ry] * inv).astype(BF16)
        attn4[ry] = attn
        delta = jnp.sum(do4[ry].astype(F32) * attn.astype(F32), axis=1, keepdims=True)
        stat[ry, 0] = top4[ry]
        stat[ry, 1] = jnp.broadcast_to(inv, (SEG, DH))
        stat[ry, 2] = jnp.broadcast_to(delta, (SEG, DH))

    half = SEG // 2
    for ry in order:
        z_part(0, ry)
    for d in (1, 3, 2):
        send(q_ref.at[:, cols(y_of[d])], q4.at[NY - d], ys.at[d - 1, 2], yr.at[NY - d - 1, 2], y_peer[d])
    lower, upper = pl.ds(0, half), pl.ds(half, half)
    arrived(fg.at[x_of[NX - 1]], xs.at[0], xr.at[0])
    send(fg.at[x_of[NX - 1], lower], fg.at[x_of[NX - 1], lower], xs.at[2], xr.at[2], x_peer[1])
    arrived(fg.at[x_of[1]], xs.at[1], xr.at[1])
    send(fg.at[x_of[1], upper], fg.at[x_of[1], upper], xs.at[3], xr.at[3], x_peer[NX - 1])
    for ry in range(NY):
        make_table(ry)
    to_smem = pltpu.make_async_copy(tab_v, tab, loc.at[0])
    to_smem.start()
    for ry in order:
        z_part(1, ry)

    arrived(fg.at[x_of[2], lower], xs.at[2], xr.at[2])
    arrived(fg.at[x_of[2], upper], xs.at[3], xr.at[3])
    width = g_ref.shape[1]
    da = dot_nt(fg[0], w_ref[:, :width])
    for i in range(1, NX):
        da += dot_nt(fg[i], w_ref[:, i * width : (i + 1) * width])
    da = da.astype(BF16)
    for i in range(NY):
        dal[i] = da[:, i * DH : (i + 1) * DH]
    do4[0] = dal[y]
    for d in (1, 3, 2):
        send(dal.at[y_of[d]], do4.at[NY - d], ds_.at[d - 1], dr.at[NY - d - 1], y_peer[d])
    for i in range(NX):
        fgt[i] = fg[i].T
    to_smem.wait()
    for ry in range(1, NY):
        arrived(q4.at[ry], ys.at[ry - 1, 2], yr.at[ry - 1, 2])
    for ry in order:
        take(0, ry)
    for ry in order:
        take(NZ - 1, ry)

    def near_step(ry, _):
        forward_near(ry)
        return _

    lax.fori_loop(0, NY, near_step, 0)
    for ry in order:
        z_part(2, ry)
    for rz in (1, NZ - 2, 2):
        for ry in order:
            take(rz, ry)
    forward_mem(0)
    forward_mem(1)
    for n, ry in enumerate(order):
        z_part(3, ry)
        take(NZ - 3, ry)
        take(3, ry)
        forward_mem(2 + n)
    for n in range(2):
        for ry in order[2 * n : 2 * n + 2]:
            z_far(ry)
        for ry in order[2 * n : 2 * n + 2]:
            take(NZ // 2, ry)
        forward_mem(6 + n)
    for ry in range(1, NY):
        arrived(do4.at[ry], ds_.at[ry - 1], dr.at[ry - 1])

    def backward_near(ry):
        q, do = q4[ry], do4[ry]
        top, inv, delta = stat[ry, 0, :, :1], stat[ry, 1, :, :1], stat[ry, 2, :, :1]
        dq = jnp.zeros((SEG, DH), F32)
        for part, at in ((0, ry), (1, cache_slot(ry))):
            weights = jnp.exp2((s_near[ry, part] - top) * scale2) * inv
            slopes = (weights * (dot_nt(do, near(at, 1)) - delta)).astype(BF16)
            dq += dot_nn(slopes, near(at, 0))
            gk_part = dot_tn(slopes, q) * scale
            gv_part = dot_tn(weights.astype(BF16), do)
            if part == 0:
                near_acc[ry, 0] = gk_part
                near_acc[ry, 1] = gv_part
            else:
                carry_out[ry, 0] = gk_part.astype(BF16)
                carry_out[ry, 1] = gv_part.astype(BF16)
        dq_acc[ry] = dq

    def backward_mem(ry):
        do = do4[ry]
        top, inv, delta = stat[ry, 0], stat[ry, 1], stat[ry, 2]
        wide_delta = jnp.concatenate([delta] * (WIDE // DH), axis=1)

        def step(n, dq):
            for i in (2 * n, 2 * n + 1):
                slopes = (p_mem[ry, i].astype(F32) * (dot_nt(do, stored(ry, i, 1)) - wide_delta)).astype(BF16)
                dq += dot_nn(slopes, stored(ry, i, 0)) * jnp.exp2((m_mem[ry, i] - top) * scale2)
            return dq

        dq = lax.fori_loop(0, CHUNKS // 2, step, jnp.zeros((SEG, DH), F32))
        gq[ry] = ((dq_acc[ry] + dq * inv) * scale).astype(BF16)

    for ry in (2, 1, 3, 0):
        finish(ry)
        if ry:
            send(attn4.at[ry], attn_in.at[y], as_.at[ry - 1], ar.at[ry - 1], y_peer[ry])
    attn_in[y] = attn4[0]

    for ry in range(NY):
        backward_near(ry)
        to = lax.rem(ry + NY - wrap, NY)
        send(carry_out.at[ry], carry_in.at[to], cs.at[ry], cr.at[to], back)

    one, two, three = y + 1 - 2 * lax.rem(y, 2), y_of[2], NY - 1 - y
    y_one, y_three = (seg_of(one, z, c), x), (seg_of(three, z, c), x)
    for d in range(1, NY):
        arrived(attn_in.at[y_of[NY - d]], as_.at[d - 1], ar.at[d - 1])
    attn = jnp.concatenate([attn_in[i] for i in range(NY)], axis=1)
    wide = attn.shape[1]
    rows = pg_ref.shape[0]
    for i in range(NY):
        part = dot_nn(fgt[i], attn).reshape(NZ, NC, rows, wide)
        pp[i] = part.astype(BF16)
        send(pp.at[i, :, 1 - c], rs0.at[i], bs.at[i], br.at[i], sibling)
    for i in range(NX):
        lo_out[i] = dot_nn(attn, w_ref[:, i * width : (i + 1) * width]).astype(BF16)
    for d in (1, 3, 2):
        send(lo_out.at[x_of[d]], lo_in.at[d - 1], ls.at[d - 1], lr.at[d - 1], x_peer[d])
    for i in range(NY):
        arrived(rs0.at[i], bs.at[i], br.at[i])
        r1[i] = (pp[i, :, c].astype(F32) + rs0[i].astype(F32)).astype(BF16)
    part_a, part_b = pl.ds(0, NZ // 2), pl.ds(NZ // 2, NZ // 2)
    send(r1.at[two, part_a], ra.at[1], rys.at[0], ryr.at[0], y_one)
    send(r1.at[two, part_b], rb.at[1], rys.at[1], ryr.at[1], y_three)
    send(r1.at[one, part_a], ra.at[0], rys.at[2], ryr.at[2], y_one)
    send(r1.at[three, part_b], rb.at[0], rys.at[3], ryr.at[3], y_three)
    backward_mem(2)
    send(gq.at[2], dq_ref.at[:, cols(y)], os_.at[0, 1], or_.at[0, 1], y_peer[2])
    arrived(ra.at[1], rys.at[0], ryr.at[0])
    ra_out[...] = (r1[three, : NZ // 2].astype(F32) + ra[1].astype(F32)).astype(BF16)
    send(ra_out, ra2, rys.at[4], ryr.at[4], y_three)
    arrived(rb.at[1], rys.at[1], ryr.at[1])
    rb_out[...] = (r1[one, NZ // 2 :].astype(F32) + rb[1].astype(F32)).astype(BF16)
    send(rb_out, rb2, rys.at[5], ryr.at[5], y_one)
    for ry in (2, 1, 3, 0):
        arrived(carry_in.at[ry], cs.at[ry], cr.at[ry])
        gk[ry] = (near_acc[ry, 0] + carry_in[ry, 0].astype(F32)).astype(BF16)
        gv[ry] = (near_acc[ry, 1] + carry_in[ry, 1].astype(F32)).astype(BF16)
        if ry:
            send(gk.at[ry], dk_ref.at[:, cols(y)], os_.at[1, ry - 1], or_.at[1, ry - 1], y_peer[ry])
            send(gv.at[ry], dv_ref.at[:, cols(y)], os_.at[2, ry - 1], or_.at[2, ry - 1], y_peer[ry])
    backward_mem(1)
    send(gq.at[1], dq_ref.at[:, cols(y)], os_.at[0, 0], or_.at[0, 0], y_peer[1])
    arrived(ra.at[0], rys.at[2], ryr.at[2])
    arrived(rb.at[0], rys.at[3], ryr.at[3])
    arrived(ra2, rys.at[4], ryr.at[4])
    r2[: NZ // 2] = (r1[y, : NZ // 2].astype(F32) + ra[0].astype(F32) + ra2[...].astype(F32)).astype(BF16)
    arrived(rb2, rys.at[5], ryr.at[5])
    r2[NZ // 2 :] = (r1[y, NZ // 2 :].astype(F32) + rb[0].astype(F32) + rb2[...].astype(F32)).astype(BF16)
    for d in (4, 3, 5, 2, 6, 1, 7):
        send(r2.at[z_of[d]], rs2.at[d - 1], rzs.at[d - 1], rzr.at[d - 1], z_peer[d])
    backward_mem(3)
    send(gq.at[3], dq_ref.at[:, cols(y)], os_.at[0, 2], or_.at[0, 2], y_peer[3])
    backward_mem(0)

    home = [
        pltpu.make_async_copy(gq.at[0], dq_ref.at[:, cols(y)], loc.at[0]),
        pltpu.make_async_copy(gk.at[0], dk_ref.at[:, cols(y)], loc.at[1]),
        pltpu.make_async_copy(gv.at[0], dv_ref.at[:, cols(y)], loc.at[2]),
    ]
    for copy in home:
        copy.start()
    out = lo_out[x].astype(F32)
    for d in range(1, NX):
        arrived(lo_in.at[d - 1], ls.at[d - 1], lr.at[d - 1])
        out += lo_in[d - 1].astype(F32)
    lo_ref[...] = out.astype(BF16)
    total = r2[z].astype(F32)
    for d in range(1, NZ):
        arrived(rs2.at[d - 1], rzs.at[d - 1], rzr.at[d - 1])
        total += rs2[d - 1].astype(F32)
    pg_ref[...] = total
    for n, ref in enumerate((dq_ref, dk_ref, dv_ref)):
        for d in range(1, NY):
            arrived(ref.at[:, cols(y_of[NY - d])], os_.at[n, d - 1], or_.at[n, d - 1])
    for copy in home:
        copy.wait()
    for copy in sends:
        copy.wait_send()


def hand_over(*refs):
    for i in range(5):
        refs[5 + i][...] = refs[i][...]


def per_device(queries, keys, values, out_grad, out_weight, retr_owner, retr_block):
    tok, wide = queries.shape
    full = out_weight.shape[1]
    rows = full // (NY * NZ * NC)
    vmem = pl.BlockSpec(memory_space=pltpu.VMEM)
    dma = pltpu.SemaphoreType.DMA
    tile = (tok, DH)
    halves = tok // BLOCK
    quarter = (NZ // 2, rows, wide)
    scratch = [
        pltpu.VMEM((NC * NZ * NY, 2, halves, BLOCK, DH), BF16),
        pltpu.VMEM((NC * NZ * NY, 2, halves, BLOCK, DH), BF16),
        pltpu.VMEM((NY,) + tile, BF16),
        pltpu.VMEM((NY,) + tile, BF16),
        pltpu.VMEM((NY,) + tile, BF16),
        pltpu.VMEM((NX, tok, wide), BF16),
        pltpu.VMEM((NX, wide, tok), BF16),
        pltpu.VMEM((NY, 2, tok, tok), F32),
        pltpu.VMEM((NY, CHUNKS, tok, WIDE), BF16),
        pltpu.VMEM((NY, CHUNKS) + tile, F32),
        pltpu.VMEM((NY,) + tile, F32),
        pltpu.VMEM((NY,) + tile, F32),
        pltpu.VMEM((NY,) + tile, F32),
        pltpu.VMEM((NY, 3) + tile, F32),
        pltpu.VMEM((NY,) + tile, BF16),
        pltpu.VMEM((NY,) + tile, BF16),
        pltpu.VMEM((NX, tok, wide), BF16),
        pltpu.VMEM((NX - 1, tok, wide), BF16),
        pltpu.VMEM((NY, NZ, NC, rows, wide), BF16),
        pltpu.VMEM((NY, NZ, rows, wide), BF16),
        pltpu.VMEM((NY, NZ, rows, wide), BF16),
        pltpu.VMEM((2,) + quarter, BF16),
        pltpu.VMEM((2,) + quarter, BF16),
        pltpu.VMEM(quarter, BF16),
        pltpu.VMEM(quarter, BF16),
        pltpu.VMEM(quarter, BF16),
        pltpu.VMEM(quarter, BF16),
        pltpu.VMEM((NZ, rows, wide), BF16),
        pltpu.VMEM((NZ - 1, rows, wide), BF16),
        pltpu.VMEM((NY,) + tile, F32),
        pltpu.VMEM((NY, 2) + tile, F32),
        pltpu.VMEM((NY, 2) + tile, BF16),
        pltpu.VMEM((NY, 2) + tile, BF16),
        pltpu.VMEM((NY,) + tile, BF16),
        pltpu.VMEM((NY,) + tile, BF16),
        pltpu.VMEM((NY,) + tile, BF16),
        pltpu.VMEM((8, DH), jnp.int32),
        pltpu.SMEM((8, DH), jnp.int32),
        dma((4,)),
        dma((NY - 1, 3)), dma((NY - 1, 3)),
        dma((4,)), dma((4,)),
        dma((2, NZ // 2, NY)), dma((2, NZ // 2, NY)),
        dma((NZ, NY)), dma((NZ, NY)),
        dma((NY - 1,)), dma((NY - 1,)),
        dma((NY - 1,)), dma((NY - 1,)),
        dma((NY,)), dma((NY,)),
        dma((NY,)), dma((NY,)),
        dma((6,)), dma((6,)),
        dma((NZ - 1,)), dma((NZ - 1,)),
        dma((NX - 1,)), dma((NX - 1,)),
        dma((3, NY - 1)), dma((3, NY - 1)),
    ]
    grad = jax.ShapeDtypeStruct((tok, wide), BF16)
    shapes = (grad, grad, grad, grad, jax.ShapeDtypeStruct((rows, wide), F32))
    results = pl.pallas_call(
        kernel,
        out_shape=shapes,
        in_specs=[vmem] * 7,
        out_specs=(vmem,) * 5,
        scratch_shapes=scratch,
        compiler_params=pltpu.CompilerParams(
            collective_id=0, has_side_effects=True, vmem_limit_bytes=60 * 1024 * 1024
        ),
    )(
        retr_owner.T,
        retr_block.T,
        queries,
        keys.reshape(halves, BLOCK, wide),
        values.reshape(halves, BLOCK, wide),
        out_grad,
        out_weight,
    )
    return pl.pallas_call(hand_over, out_shape=shapes, in_specs=[vmem] * 5, out_specs=(vmem,) * 5)(*results)


def solution(mesh):
    rows = P("seg", "head")
    return jax.shard_map(
        per_device,
        mesh=mesh,
        in_specs=(rows, rows, rows, rows, P("head", None), P(), P()),
        out_specs=(rows,) * 5,
        check_vma=False,
    )
```

time: 124 us -> 92.3 us (0.74)
  Pallas kernels: 113 us -> 90.5 us
  local copies, waits for them, and re-layouts: 10.2 us -> 0 us
    pallas_call x1 -> x2, Pallas kernels: 113 us -> 90.5 us  [the longest x1 88.4 us: per_device(): pl.pallas_call(kernel, out_shape=shapes, in_specs=[vmem] * 7, out_specs=(...]
    unnamed x9 -> x0, local copies, waits for them, and re-layouts: 10.2 us -> none
where the time goes in v2:
time: 92.3 us; the launch traced here: 91.2 us
  Pallas kernels  90.5 us (98%)
    pallas_call x1, Pallas kernels, per_device(): pl.pallas_call(kernel, out_shape=shapes, in_specs=[vmem] * 7, out_specs=(...  88.4 us
    pallas_call x1, Pallas kernels, per_device(): pl.pallas_call(hand_over, out_shape=shapes, in_specs=[vmem] * 5, out_spec...  2.18 us

profile of v2, /device:TPU:1, one launch (start us, length us, event | category | flops | bytes accessed | tf_op | source)
XLA Modules:
  0.0 91.2 jit_solution(95005285102657686)
XLA Ops:
  0.6 88.4 %shard_map.110 = (bf16[256,512]{1,0:T(8,128)(2,1)}, bf16[256,512]{1,0:T(8,128)(2,1)}, bf16[256,512]{1,0:T(8,128)(2,1)}, bf16[256,512]{1,0:T(8,128)(2,1)}, f32[32,512]{1,0:T(8,128)}) custom-call(s32[32,64]{1,0:T(8,128)} %bitcast.6, s32[32,64]{1,0:T(8,128)} %bitcast.7, bf16[256,512]{1,0:T(8,128)(2,1)} %q_ref.1, bf16[2,128,512]{2,1,0:T(8,128)(2,1)} %bitcast.4, ...), custom_call_target="tpu_custom_call" | custom-call | tf_op jit(solution)/shard_map/pallas_call | solution.py:492
  89.0 2.2 %shard_map.111 = (bf16[256,512]{1,0:T(8,128)(2,1)}, bf16[256,512]{1,0:T(8,128)(2,1)}, bf16[256,512]{1,0:T(8,128)(2,1)}, bf16[256,512]{1,0:T(8,128)(2,1)}, f32[32,512]{1,0:T(8,128)}) custom-call(bf16[256,512]{1,0:T(8,128)(2,1)} %get-tuple-element.10.refs_0_, bf16[256,512]{1,0:T(8,128)(2,1)} %get-tuple-element.11.refs_1_, ...), custom_call_target="tpu_custom_call" | custom-call | tf_op jit(solution)/shard_map/pallas_call | solution.py:510

commit v3 on v2

--- a/solution.py
+++ b/solution.py
@@ -36,10 +36,9 @@
 def kernel(
     owner_ref, block_ref, q_ref, k_ref, v_ref, g_ref, w_ref,
     lo_ref, dq_ref, dk_ref, dv_ref, pg_ref,
-    kv, kvc, q4, do4, dal, fg, fgt, s_near, p_mem, m_mem, top4, sum4, mix4, stat, attn4, attn_in, lo_out, lo_in,
-    pp, rs0, r1, ra, rb, ra_out, rb_out, ra2, rb2, r2, rs2, dq_acc, near_acc, carry_out, carry_in, gq, gk, gv,
-    tab_v, tab,
-    loc, ys, yr, xs, xr, zs, zr, ms, mr, ds_, dr, as_, ar, cs, cr, bs, br, rys, ryr, rzs, rzr, ls, lr, os_, or_,
+    w_v, lo_v, kv, kvc, q4, do4, g4, s_near, p_mem, m_mem, top4, sum4, mix4, stat, attn4, attn_in, lo_out, lo_in,
+    pt, pp, rs0, r1, rs2, r2, dq_acc, near_acc, carry_out, carry_in, gq, gk, gv, tab_v, tab,
+    loc, ys, yr, gs, gr, xs, xr, zs, zr, ms, mr, as_, ar, bs, br, cs, cr, rzs, rzr, ls, lr, ps, pr, os_, or_,
 ):
     s_me = lax.axis_index("seg")
     x = lax.axis_index("head")
@@ -87,9 +86,10 @@
         pltpu.make_async_copy(k_ref.at[:, :, cols(y)], kv.at[0, 0], loc.at[0]),
         pltpu.make_async_copy(v_ref.at[:, :, cols(y)], kv.at[0, 1], loc.at[1]),
         pltpu.make_async_copy(q_ref.at[:, cols(y)], q4.at[0], loc.at[2]),
-        pltpu.make_async_copy(g_ref, fg.at[x], loc.at[3]),
+        pltpu.make_async_copy(g_ref, g4.at[0, x], loc.at[3]),
     ]
-    for copy in own:
+    weights_in = pltpu.make_async_copy(w_ref, w_v, loc.at[4])
+    for copy in own + [weights_in]:
         copy.start()
 
     barrier = pltpu.get_barrier_semaphore()
@@ -101,8 +101,8 @@
     for d in (1, 3, 2):
         send(k_ref.at[:, :, cols(y_of[d])], kv.at[NY - d, 0], ys.at[d - 1, 0], yr.at[NY - d - 1, 0], y_peer[d])
         send(v_ref.at[:, :, cols(y_of[d])], kv.at[NY - d, 1], ys.at[d - 1, 1], yr.at[NY - d - 1, 1], y_peer[d])
-    send(g_ref, fg.at[x], xs.at[0], xr.at[0], x_peer[1])
-    send(g_ref, fg.at[x], xs.at[1], xr.at[1], x_peer[NX - 1])
+    send(g_ref, g4.at[0, x], xs.at[0, 0], xr.at[0, 0], x_peer[1])
+    send(g_ref, g4.at[0, x], xs.at[0, 1], xr.at[0, 1], x_peer[NX - 1])
     for copy in own:
         copy.wait()
     order = (0, 1, 3, 2)
@@ -234,37 +234,55 @@
         stat[ry, 1] = jnp.broadcast_to(inv, (SEG, DH))
         stat[ry, 2] = jnp.broadcast_to(delta, (SEG, DH))
 
-    half = SEG // 2
-    for ry in order:
-        z_part(0, ry)
+    lower, upper = pl.ds(0, SEG // 2), pl.ds(SEG // 2, SEG // 2)
+    width = g4.shape[3]
+
+    def x_first(ry):
+        arrived(g4.at[ry, x], gs.at[ry - 1], gr.at[ry - 1])
+        send(g4.at[ry, x], g4.at[ry, x], xs.at[ry, 0], xr.at[ry, 0], x_peer[1])
+        send(g4.at[ry, x], g4.at[ry, x], xs.at[ry, 1], xr.at[ry, 1], x_peer[NX - 1])
+
+    def x_second(ry):
+        left, right = x_of[NX - 1], x_of[1]
+        arrived(g4.at[ry, left], xs.at[ry, 0], xr.at[ry, 0])
+        send(g4.at[ry, left, lower], g4.at[ry, left, lower], xs.at[ry, 2], xr.at[ry, 2], x_peer[1])
+        arrived(g4.at[ry, right], xs.at[ry, 1], xr.at[ry, 1])
+        send(g4.at[ry, right, upper], g4.at[ry, right, upper], xs.at[ry, 3], xr.at[ry, 3], x_peer[NX - 1])
+
+    def d_attn(ry):
+        arrived(g4.at[ry, x_of[2], lower], xs.at[ry, 2], xr.at[ry, 2])
+        arrived(g4.at[ry, x_of[2], upper], xs.at[ry, 3], xr.at[ry, 3])
+        da = jnp.zeros((SEG, DH), F32)
+        for i in range(NX):
+            da += dot_nt(g4[ry, i], w_v[cols(y), i * width : (i + 1) * width])
+        do4[ry] = da.astype(BF16)
+
+    def g_send(d):
+        send(g_ref, g4.at[NY - d, x], gs.at[d - 1], gr.at[NY - d - 1], y_peer[d])
+
+    z_part(0, order[0])
+    z_part(0, order[1])
+    g_send(3)
+    z_part(0, order[2])
+    g_send(1)
+    g_send(2)
     for d in (1, 3, 2):
         send(q_ref.at[:, cols(y_of[d])], q4.at[NY - d], ys.at[d - 1, 2], yr.at[NY - d - 1, 2], y_peer[d])
-    lower, upper = pl.ds(0, half), pl.ds(half, half)
-    arrived(fg.at[x_of[NX - 1]], xs.at[0], xr.at[0])
-    send(fg.at[x_of[NX - 1], lower], fg.at[x_of[NX - 1], lower], xs.at[2], xr.at[2], x_peer[1])
-    arrived(fg.at[x_of[1]], xs.at[1], xr.at[1])
-    send(fg.at[x_of[1], upper], fg.at[x_of[1], upper], xs.at[3], xr.at[3], x_peer[NX - 1])
+    z_part(0, order[3])
     for ry in range(NY):
         make_table(ry)
     to_smem = pltpu.make_async_copy(tab_v, tab, loc.at[0])
     to_smem.start()
-    for ry in order:
-        z_part(1, ry)
-
-    arrived(fg.at[x_of[2], lower], xs.at[2], xr.at[2])
-    arrived(fg.at[x_of[2], upper], xs.at[3], xr.at[3])
-    width = g_ref.shape[1]
-    da = dot_nt(fg[0], w_ref[:, :width])
-    for i in range(1, NX):
-        da += dot_nt(fg[i], w_ref[:, i * width : (i + 1) * width])
-    da = da.astype(BF16)
-    for i in range(NY):
-        dal[i] = da[:, i * DH : (i + 1) * DH]
-    do4[0] = dal[y]
-    for d in (1, 3, 2):
-        send(dal.at[y_of[d]], do4.at[NY - d], ds_.at[d - 1], dr.at[NY - d - 1], y_peer[d])
-    for i in range(NX):
-        fgt[i] = fg[i].T
+    z_part(1, order[0])
+    x_second(0)
+    z_part(1, order[1])
+    x_first(1)
+    z_part(1, order[2])
+    x_first(3)
+    z_part(1, order[3])
+    x_first(2)
+    weights_in.wait()
+    d_attn(0)
     to_smem.wait()
     for ry in range(1, NY):
         arrived(q4.at[ry], ys.at[ry - 1, 2], yr.at[ry - 1, 2])
@@ -278,26 +296,36 @@
         return _
 
     lax.fori_loop(0, NY, near_step, 0)
-    for ry in order:
-        z_part(2, ry)
+    z_part(2, order[0])
+    z_part(2, order[1])
+    x_second(1)
+    z_part(2, order[2])
+    z_part(2, order[3])
     for rz in (1, NZ - 2, 2):
         for ry in order:
             take(rz, ry)
+    x_second(3)
     forward_mem(0)
     forward_mem(1)
     for n, ry in enumerate(order):
         z_part(3, ry)
         take(NZ - 3, ry)
         take(3, ry)
+        if n == 0:
+            x_second(2)
         forward_mem(2 + n)
+        if n == 0:
+            d_attn(1)
+        if n == 1:
+            d_attn(3)
     for n in range(2):
         for ry in order[2 * n : 2 * n + 2]:
             z_far(ry)
         for ry in order[2 * n : 2 * n + 2]:
             take(NZ // 2, ry)
         forward_mem(6 + n)
-    for ry in range(1, NY):
-        arrived(do4.at[ry], ds_.at[ry - 1], dr.at[ry - 1])
+        if n == 0:
+            d_attn(2)
 
     def backward_near(ry):
         q, do = q4[ry], do4[ry]
@@ -323,56 +351,47 @@
         wide_delta = jnp.concatenate([delta] * (WIDE // DH), axis=1)
 
         def step(n, dq):
-            for i in (2 * n, 2 * n + 1):
+            for i in [4 * n + k for k in range(4)]:
                 slopes = (p_mem[ry, i].astype(F32) * (dot_nt(do, stored(ry, i, 1)) - wide_delta)).astype(BF16)
                 dq += dot_nn(slopes, stored(ry, i, 0)) * jnp.exp2((m_mem[ry, i] - top) * scale2)
             return dq
 
-        dq = lax.fori_loop(0, CHUNKS // 2, step, jnp.zeros((SEG, DH), F32))
+        dq = lax.fori_loop(0, CHUNKS // 4, step, jnp.zeros((SEG, DH), F32))
         gq[ry] = ((dq_acc[ry] + dq * inv) * scale).astype(BF16)
 
-    for ry in (2, 1, 3, 0):
+    for n, ry in enumerate((2, 1, 3, 0)):
         finish(ry)
         if ry:
             send(attn4.at[ry], attn_in.at[y], as_.at[ry - 1], ar.at[ry - 1], y_peer[ry])
+        turned = attn4[ry].T
+        for i in range(NX):
+            part = dot_nn(turned, g4[ry, i])
+            pt[i] = part if n == 0 else pt[i] + part
     attn_in[y] = attn4[0]
 
+    rows = pg_ref.shape[0]
+    for i in range(NY):
+        pp[i] = pt[i].T.astype(BF16).reshape(NZ, NC, rows, DH)
+        send(pp.at[i, :, 1 - c], rs0.at[i], bs.at[i], br.at[i], sibling)
     for ry in range(NY):
         backward_near(ry)
         to = lax.rem(ry + NY - wrap, NY)
         send(carry_out.at[ry], carry_in.at[to], cs.at[ry], cr.at[to], back)
-
-    one, two, three = y + 1 - 2 * lax.rem(y, 2), y_of[2], NY - 1 - y
-    y_one, y_three = (seg_of(one, z, c), x), (seg_of(three, z, c), x)
-    for d in range(1, NY):
+    for i in range(NY):
+        arrived(rs0.at[i], bs.at[i], br.at[i])
+        r1[:, i] = (pp[i, :, c].astype(F32) + rs0[i].astype(F32)).astype(BF16)
+    for d in (4, 3, 5, 2, 6, 1, 7):
+        send(r1.at[z_of[d]], rs2.at[d - 1], rzs.at[d - 1], rzr.at[d - 1], z_peer[d])
+
+    for d in (1, 3, 2):
         arrived(attn_in.at[y_of[NY - d]], as_.at[d - 1], ar.at[d - 1])
     attn = jnp.concatenate([attn_in[i] for i in range(NY)], axis=1)
-    wide = attn.shape[1]
-    rows = pg_ref.shape[0]
-    for i in range(NY):
-        part = dot_nn(fgt[i], attn).reshape(NZ, NC, rows, wide)
-        pp[i] = part.astype(BF16)
-        send(pp.at[i, :, 1 - c], rs0.at[i], bs.at[i], br.at[i], sibling)
     for i in range(NX):
-        lo_out[i] = dot_nn(attn, w_ref[:, i * width : (i + 1) * width]).astype(BF16)
-    for d in (1, 3, 2):
+        lo_out[i] = dot_nn(attn, w_v[:, i * width : (i + 1) * width]).astype(BF16)
+    for d in (2, 1, 3):
         send(lo_out.at[x_of[d]], lo_in.at[d - 1], ls.at[d - 1], lr.at[d - 1], x_peer[d])
-    for i in range(NY):
-        arrived(rs0.at[i], bs.at[i], br.at[i])
-        r1[i] = (pp[i, :, c].astype(F32) + rs0[i].astype(F32)).astype(BF16)
-    part_a, part_b = pl.ds(0, NZ // 2), pl.ds(NZ // 2, NZ // 2)
-    send(r1.at[two, part_a], ra.at[1], rys.at[0], ryr.at[0], y_one)
-    send(r1.at[two, part_b], rb.at[1], rys.at[1], ryr.at[1], y_three)
-    send(r1.at[one, part_a], ra.at[0], rys.at[2], ryr.at[2], y_one)
-    send(r1.at[three, part_b], rb.at[0], rys.at[3], ryr.at[3], y_three)
     backward_mem(2)
     send(gq.at[2], dq_ref.at[:, cols(y)], os_.at[0, 1], or_.at[0, 1], y_peer[2])
-    arrived(ra.at[1], rys.at[0], ryr.at[0])
-    ra_out[...] = (r1[three, : NZ // 2].astype(F32) + ra[1].astype(F32)).astype(BF16)
-    send(ra_out, ra2, rys.at[4], ryr.at[4], y_three)
-    arrived(rb.at[1], rys.at[1], ryr.at[1])
-    rb_out[...] = (r1[one, NZ // 2 :].astype(F32) + rb[1].astype(F32)).astype(BF16)
-    send(rb_out, rb2, rys.at[5], ryr.at[5], y_one)
     for ry in (2, 1, 3, 0):
         arrived(carry_in.at[ry], cs.at[ry], cr.at[ry])
         gk[ry] = (near_acc[ry, 0] + carry_in[ry, 0].astype(F32)).astype(BF16)
@@ -382,14 +401,13 @@
             send(gv.at[ry], dv_ref.at[:, cols(y)], os_.at[2, ry - 1], or_.at[2, ry - 1], y_peer[ry])
     backward_mem(1)
     send(gq.at[1], dq_ref.at[:, cols(y)], os_.at[0, 0], or_.at[0, 0], y_peer[1])
-    arrived(ra.at[0], rys.at[2], ryr.at[2])
-    arrived(rb.at[0], rys.at[3], ryr.at[3])
-    arrived(ra2, rys.at[4], ryr.at[4])
-    r2[: NZ // 2] = (r1[y, : NZ // 2].astype(F32) + ra[0].astype(F32) + ra2[...].astype(F32)).astype(BF16)
-    arrived(rb2, rys.at[5], ryr.at[5])
-    r2[NZ // 2 :] = (r1[y, NZ // 2 :].astype(F32) + rb[0].astype(F32) + rb2[...].astype(F32)).astype(BF16)
-    for d in (4, 3, 5, 2, 6, 1, 7):
-        send(r2.at[z_of[d]], rs2.at[d - 1], rzs.at[d - 1], rzr.at[d - 1], z_peer[d])
+    total = r1[z].astype(F32)
+    for d in range(1, NZ):
+        arrived(rs2.at[d - 1], rzs.at[d - 1], rzr.at[d - 1])
+        total += rs2[d - 1].astype(F32)
+    r2[...] = total
+    for d in (2, 1, 3):
+        send(r2.at[y_of[d]], pg_ref.at[:, cols(y)], ps.at[d - 1], pr.at[d - 1], y_peer[d])
     backward_mem(3)
     send(gq.at[3], dq_ref.at[:, cols(y)], os_.at[0, 2], or_.at[0, 2], y_peer[3])
     backward_mem(0)
@@ -398,6 +416,7 @@
         pltpu.make_async_copy(gq.at[0], dq_ref.at[:, cols(y)], loc.at[0]),
         pltpu.make_async_copy(gk.at[0], dk_ref.at[:, cols(y)], loc.at[1]),
         pltpu.make_async_copy(gv.at[0], dv_ref.at[:, cols(y)], loc.at[2]),
+        pltpu.make_async_copy(r2.at[y], pg_ref.at[:, cols(y)], loc.at[5]),
     ]
     for copy in home:
         copy.start()
@@ -405,12 +424,11 @@
     for d in range(1, NX):
         arrived(lo_in.at[d - 1], ls.at[d - 1], lr.at[d - 1])
         out += lo_in[d - 1].astype(F32)
-    lo_ref[...] = out.astype(BF16)
-    total = r2[z].astype(F32)
-    for d in range(1, NZ):
-        arrived(rs2.at[d - 1], rzs.at[d - 1], rzr.at[d - 1])
-        total += rs2[d - 1].astype(F32)
-    pg_ref[...] = total
+    lo_v[...] = out.astype(BF16)
+    home.append(pltpu.make_async_copy(lo_v, lo_ref, loc.at[3]))
+    home[-1].start()
+    for d in range(1, NY):
+        arrived(pg_ref.at[:, cols(y_of[NY - d])], ps.at[d - 1], pr.at[d - 1])
     for n, ref in enumerate((dq_ref, dk_ref, dv_ref)):
         for d in range(1, NY):
             arrived(ref.at[:, cols(y_of[NY - d])], os_.at[n, d - 1], or_.at[n, d - 1])
@@ -430,18 +448,18 @@
     full = out_weight.shape[1]
     rows = full // (NY * NZ * NC)
     vmem = pl.BlockSpec(memory_space=pltpu.VMEM)
+    anywhere = pl.BlockSpec(memory_space=pl.ANY)
     dma = pltpu.SemaphoreType.DMA
     tile = (tok, DH)
     halves = tok // BLOCK
-    quarter = (NZ // 2, rows, wide)
     scratch = [
+        pltpu.VMEM((wide, full), BF16),
+        pltpu.VMEM((tok, wide), BF16),
         pltpu.VMEM((NC * NZ * NY, 2, halves, BLOCK, DH), BF16),
         pltpu.VMEM((NC * NZ * NY, 2, halves, BLOCK, DH), BF16),
         pltpu.VMEM((NY,) + tile, BF16),
         pltpu.VMEM((NY,) + tile, BF16),
-        pltpu.VMEM((NY,) + tile, BF16),
-        pltpu.VMEM((NX, tok, wide), BF16),
-        pltpu.VMEM((NX, wide, tok), BF16),
+        pltpu.VMEM((NY, NX, tok, wide), BF16),
         pltpu.VMEM((NY, 2, tok, tok), F32),
         pltpu.VMEM((NY, CHUNKS, tok, WIDE), BF16),
         pltpu.VMEM((NY, CHUNKS) + tile, F32),
@@ -453,17 +471,12 @@
         pltpu.VMEM((NY,) + tile, BF16),
         pltpu.VMEM((NX, tok, wide), BF16),
         pltpu.VMEM((NX - 1, tok, wide), BF16),
-        pltpu.VMEM((NY, NZ, NC, rows, wide), BF16),
-        pltpu.VMEM((NY, NZ, rows, wide), BF16),
-        pltpu.VMEM((NY, NZ, rows, wide), BF16),
-        pltpu.VMEM((2,) + quarter, BF16),
-        pltpu.VMEM((2,) + quarter, BF16),
-        pltpu.VMEM(quarter, BF16),
-        pltpu.VMEM(quarter, BF16),
-        pltpu.VMEM(quarter, BF16),
-        pltpu.VMEM(quarter, BF16),
-        pltpu.VMEM((NZ, rows, wide), BF16),
-        pltpu.VMEM((NZ - 1, rows, wide), BF16),
+        pltpu.VMEM((NX, DH, wide), F32),
+        pltpu.VMEM((NY, NZ, NC, rows, DH), BF16),
+        pltpu.VMEM((NY, NZ, rows, DH), BF16),
+        pltpu.VMEM((NZ, NY, rows, DH), BF16),
+        pltpu.VMEM((NZ - 1, NY, rows, DH), BF16),
+        pltpu.VMEM((NY, rows, DH), F32),
         pltpu.VMEM((NY,) + tile, F32),
         pltpu.VMEM((NY, 2) + tile, F32),
         pltpu.VMEM((NY, 2) + tile, BF16),
@@ -473,18 +486,18 @@
         pltpu.VMEM((NY,) + tile, BF16),
         pltpu.VMEM((8, DH), jnp.int32),
         pltpu.SMEM((8, DH), jnp.int32),
-        dma((4,)),
+        dma((6,)),
         dma((NY - 1, 3)), dma((NY - 1, 3)),
-        dma((4,)), dma((4,)),
+        dma((NY - 1,)), dma((NY - 1,)),
+        dma((NY, 4)), dma((NY, 4)),
         dma((2, NZ // 2, NY)), dma((2, NZ // 2, NY)),
         dma((NZ, NY)), dma((NZ, NY)),
         dma((NY - 1,)), dma((NY - 1,)),
-        dma((NY - 1,)), dma((NY - 1,)),
         dma((NY,)), dma((NY,)),
         dma((NY,)), dma((NY,)),
-        dma((6,)), dma((6,)),
         dma((NZ - 1,)), dma((NZ - 1,)),
         dma((NX - 1,)), dma((NX - 1,)),
+        dma((NY - 1,)), dma((NY - 1,)),
         dma((3, NY - 1)), dma((3, NY - 1)),
     ]
     grad = jax.ShapeDtypeStruct((tok, wide), BF16)
@@ -492,8 +505,8 @@
     results = pl.pallas_call(
         kernel,
         out_shape=shapes,
-        in_specs=[vmem] * 7,
-        out_specs=(vmem,) * 5,
+        in_specs=[vmem] * 2 + [anywhere] * 5,
+        out_specs=(anywhere,) * 5,
         scratch_shapes=scratch,
         compiler_params=pltpu.CompilerParams(
             collective_id=0, has_side_effects=True, vmem_limit_bytes=60 * 1024 * 1024

time: 92.3 us -> 87.3 us (0.946)
  Pallas kernels: 90.5 us -> 86.4 us
    pallas_call x1, Pallas kernels: 88.4 us -> 84.2 us  [per_device(): pl.pallas_call(kernel, out_shape=shapes, in_specs=[vmem] * 2 + [anywhere]...]
where the time goes in v3:
time: 87.3 us; the launch traced here: 87.1 us
  Pallas kernels  86.4 us (99%)
    pallas_call x1, Pallas kernels, per_device(): pl.pallas_call(kernel, out_shape=shapes, in_specs=[vmem] * 2 + [anywhere]...  84.2 us
    pallas_call x1, Pallas kernels, per_device(): pl.pallas_call(hand_over, out_shape=shapes, in_specs=[vmem] * 5, out_spec...  2.18 us

profile of v3, /device:TPU:1, one launch (start us, length us, event | category | flops | bytes accessed | tf_op | source)
XLA Modules:
  0.0 87.1 jit_solution(14057567552853124926)
XLA Ops:
  0.6 84.2 %shard_map.110 = (bf16[256,512]{1,0:T(8,128)(2,1)}, bf16[256,512]{1,0:T(8,128)(2,1)}, bf16[256,512]{1,0:T(8,128)(2,1)}, bf16[256,512]{1,0:T(8,128)(2,1)}, f32[32,512]{1,0:T(8,128)}) custom-call(s32[32,64]{1,0:T(8,128)} %bitcast.6, s32[32,64]{1,0:T(8,128)} %bitcast.7, bf16[256,512]{1,0:T(8,128)(2,1)} %q_ref.1, bf16[2,128,512]{2,1,0:T(8,128)(2,1)} %bitcast.4, ...), custom_call_target="tpu_custom_call" | custom-call | tf_op jit(solution)/shard_map/pallas_call | solution.py:505
  84.9 2.2 %shard_map.111 = (bf16[256,512]{1,0:T(8,128)(2,1)}, bf16[256,512]{1,0:T(8,128)(2,1)}, bf16[256,512]{1,0:T(8,128)(2,1)}, bf16[256,512]{1,0:T(8,128)(2,1)}, f32[32,512]{1,0:T(8,128)}) custom-call(bf16[256,512]{1,0:T(8,128)(2,1)} %get-tuple-element.10.refs_0_, bf16[256,512]{1,0:T(8,128)(2,1)} %get-tuple-element.11.refs_1_, ...), custom_call_target="tpu_custom_call" | custom-call | tf_op jit(solution)/shard_map/pallas_call | solution.py:523

commit v4 on v3

--- a/solution.py
+++ b/solution.py
@@ -260,29 +260,28 @@
     def g_send(d):
         send(g_ref, g4.at[NY - d, x], gs.at[d - 1], gr.at[NY - d - 1], y_peer[d])
 
-    z_part(0, order[0])
-    z_part(0, order[1])
-    g_send(3)
-    z_part(0, order[2])
-    g_send(1)
-    g_send(2)
+    z_part(0, 0)
+    z_part(1, 0)
+    z_part(0, 1)
+    z_part(0, 3)
+    for d in (3, 1, 2):
+        g_send(d)
+    x_second(0)
+    z_part(0, 2)
     for d in (1, 3, 2):
         send(q_ref.at[:, cols(y_of[d])], q4.at[NY - d], ys.at[d - 1, 2], yr.at[NY - d - 1, 2], y_peer[d])
-    z_part(0, order[3])
+    z_part(2, 0)
     for ry in range(NY):
         make_table(ry)
     to_smem = pltpu.make_async_copy(tab_v, tab, loc.at[0])
     to_smem.start()
-    z_part(1, order[0])
-    x_second(0)
-    z_part(1, order[1])
+    z_part(1, 1)
+    weights_in.wait()
+    z_part(1, 3)
+    d_attn(0)
+    z_part(1, 2)
     x_first(1)
-    z_part(1, order[2])
     x_first(3)
-    z_part(1, order[3])
-    x_first(2)
-    weights_in.wait()
-    d_attn(0)
     to_smem.wait()
     for ry in range(1, NY):
         arrived(q4.at[ry], ys.at[ry - 1, 2], yr.at[ry - 1, 2])
@@ -296,36 +295,49 @@
         return _
 
     lax.fori_loop(0, NY, near_step, 0)
-    z_part(2, order[0])
-    z_part(2, order[1])
+    z_part(3, 0)
+    z_part(2, 1)
+    x_first(2)
+    z_part(2, 3)
     x_second(1)
-    z_part(2, order[2])
-    z_part(2, order[3])
-    for rz in (1, NZ - 2, 2):
+    for ry in order:
+        take(1, ry)
+    z_part(2, 2)
+    for rz in (NZ - 2, 2):
         for ry in order:
             take(rz, ry)
+    forward_mem(0)
     x_second(3)
-    forward_mem(0)
+    z_far(0)
     forward_mem(1)
-    for n, ry in enumerate(order):
-        z_part(3, ry)
-        take(NZ - 3, ry)
-        take(3, ry)
-        if n == 0:
-            x_second(2)
-        forward_mem(2 + n)
-        if n == 0:
-            d_attn(1)
-        if n == 1:
-            d_attn(3)
-    for n in range(2):
-        for ry in order[2 * n : 2 * n + 2]:
-            z_far(ry)
-        for ry in order[2 * n : 2 * n + 2]:
-            take(NZ // 2, ry)
-        forward_mem(6 + n)
-        if n == 0:
-            d_attn(2)
+    take(NZ - 3, 0)
+    take(3, 0)
+    z_part(3, 1)
+    forward_mem(2)
+    take(NZ - 3, 1)
+    take(3, 1)
+    z_part(3, 3)
+    forward_mem(3)
+    take(NZ - 3, 3)
+    take(3, 3)
+    x_second(2)
+    d_attn(1)
+    z_part(3, 2)
+    forward_mem(4)
+    take(NZ - 3, 2)
+    take(3, 2)
+    z_far(1)
+    forward_mem(5)
+    take(NZ // 2, 0)
+    take(NZ // 2, 1)
+    z_far(3)
+    d_attn(3)
+    z_far(2)
+    forward_mem(6)
+    d_attn(2)
+    take(NZ // 2, 3)
+    take(NZ // 2, 2)
+    forward_mem(7)
 
     def backward_near(ry):
         q, do = q4[ry], do4[ry]

time: 87.3 us -> 84.2 us (0.964)
  Pallas kernels: 86.4 us -> 83.3 us
    pallas_call x1, Pallas kernels: 84.2 us -> 81.2 us  [per_device(): pl.pallas_call(kernel, out_shape=shapes, in_specs=[vmem] * 2 + [anywhere]...]
where the time goes in v4:
time: 84.2 us; the launch traced here: 84 us
  Pallas kernels  83.3 us (99%)
    pallas_call x1, Pallas kernels, per_device(): pl.pallas_call(kernel, out_shape=shapes, in_specs=[vmem] * 2 + [anywhere]...  81.2 us
    pallas_call x1, Pallas kernels, per_device(): pl.pallas_call(hand_over, out_shape=shapes, in_specs=[vmem] * 5, out_spec...  2.18 us

profile of v4, /device:TPU:1, one launch (start us, length us, event | category | flops | bytes accessed | tf_op | source)
XLA Modules:
  0.0 84.0 jit_solution(1753645487221715543)
XLA Ops:
  0.6 81.2 %shard_map.110 = (bf16[256,512]{1,0:T(8,128)(2,1)}, bf16[256,512]{1,0:T(8,128)(2,1)}, bf16[256,512]{1,0:T(8,128)(2,1)}, bf16[256,512]{1,0:T(8,128)(2,1)}, f32[32,512]{1,0:T(8,128)}) custom-call(s32[32,64]{1,0:T(8,128)} %bitcast.6, s32[32,64]{1,0:T(8,128)} %bitcast.7, bf16[256,512]{1,0:T(8,128)(2,1)} %q_ref.1, bf16[2,128,512]{2,1,0:T(8,128)(2,1)} %bitcast.4, ...), custom_call_target="tpu_custom_call" | custom-call | tf_op jit(solution)/shard_map/pallas_call | solution.py:517
  81.8 2.2 %shard_map.111 = (bf16[256,512]{1,0:T(8,128)(2,1)}, bf16[256,512]{1,0:T(8,128)(2,1)}, bf16[256,512]{1,0:T(8,128)(2,1)}, bf16[256,512]{1,0:T(8,128)(2,1)}, f32[32,512]{1,0:T(8,128)}) custom-call(bf16[256,512]{1,0:T(8,128)(2,1)} %get-tuple-element.10.refs_0_, bf16[256,512]{1,0:T(8,128)(2,1)} %get-tuple-element.11.refs_1_, ...), custom_call_target="tpu_custom_call" | custom-call | tf_op jit(solution)/shard_map/pallas_call | solution.py:535

commit v5 on v4

--- a/solution.py
+++ b/solution.py
@@ -37,7 +37,7 @@
     owner_ref, block_ref, q_ref, k_ref, v_ref, g_ref, w_ref,
     lo_ref, dq_ref, dk_ref, dv_ref, pg_ref,
     w_v, lo_v, kv, kvc, q4, do4, g4, s_near, p_mem, m_mem, top4, sum4, mix4, stat, attn4, attn_in, lo_out, lo_in,
-    pt, pp, rs0, r1, rs2, r2, dq_acc, near_acc, carry_out, carry_in, gq, gk, gv, tab_v, tab,
+    pp, rs0, r1, rs2, r2, dq_acc, near_acc, carry_out, carry_in, gq, gk, gv, tab_v, tab,
     loc, ys, yr, gs, gr, xs, xr, zs, zr, ms, mr, as_, ar, bs, br, cs, cr, rzs, rzr, ls, lr, ps, pr, os_, or_,
 ):
     s_me = lax.axis_index("seg")
@@ -364,26 +364,24 @@
 
         def step(n, dq):
             for i in [4 * n + k for k in range(4)]:
-                slopes = (p_mem[ry, i].astype(F32) * (dot_nt(do, stored(ry, i, 1)) - wide_delta)).astype(BF16)
+                slopes = p_mem[ry, i] * (dot_nt(do, stored(ry, i, 1)) - wide_delta).astype(BF16)
                 dq += dot_nn(slopes, stored(ry, i, 0)) * jnp.exp2((m_mem[ry, i] - top) * scale2)
             return dq
 
         dq = lax.fori_loop(0, CHUNKS // 4, step, jnp.zeros((SEG, DH), F32))
         gq[ry] = ((dq_acc[ry] + dq * inv) * scale).astype(BF16)
 
-    for n, ry in enumerate((2, 1, 3, 0)):
+    for ry in (2, 1, 3, 0):
         finish(ry)
         if ry:
             send(attn4.at[ry], attn_in.at[y], as_.at[ry - 1], ar.at[ry - 1], y_peer[ry])
-        turned = attn4[ry].T
-        for i in range(NX):
-            part = dot_nn(turned, g4[ry, i])
-            pt[i] = part if n == 0 else pt[i] + part
     attn_in[y] = attn4[0]
 
     rows = pg_ref.shape[0]
+    turned = jnp.concatenate([attn4[ry].T for ry in range(NY)], axis=1)
     for i in range(NY):
-        pp[i] = pt[i].T.astype(BF16).reshape(NZ, NC, rows, DH)
+        part = dot_nn(turned, g4[:, i].reshape(NY * SEG, width))
+        pp[i] = part.T.astype(BF16).reshape(NZ, NC, rows, DH)
         send(pp.at[i, :, 1 - c], rs0.at[i], bs.at[i], br.at[i], sibling)
     for ry in range(NY):
         backward_near(ry)
@@ -483,7 +481,6 @@
         pltpu.VMEM((NY,) + tile, BF16),
         pltpu.VMEM((NX, tok, wide), BF16),
         pltpu.VMEM((NX - 1, tok, wide), BF16),
-        pltpu.VMEM((NX, DH, wide), F32),
         pltpu.VMEM((NY, NZ, NC, rows, DH), BF16),
         pltpu.VMEM((NY, NZ, rows, DH), BF16),
         pltpu.VMEM((NZ, NY, rows, DH), BF16),

time: 84.2 us -> 84.4 us (level)
  no operation moved by 1% of the time
where the time goes in v5:
time: 84.4 us; the launch traced here: 84.1 us
  Pallas kernels  83.4 us (99%)
    pallas_call x1, Pallas kernels, per_device(): pl.pallas_call(kernel, out_shape=shapes, in_specs=[vmem] * 2 + [anywhere]...  81.3 us
    pallas_call x1, Pallas kernels, per_device(): pl.pallas_call(hand_over, out_shape=shapes, in_specs=[vmem] * 5, out_spec...  2.18 us

profile of v5, /device:TPU:1, one launch (start us, length us, event | category | flops | bytes accessed | tf_op | source)
XLA Modules:
  0.0 84.1 jit_solution(10565717403246592817)
XLA Ops:
  0.6 81.3 %shard_map.110 = (bf16[256,512]{1,0:T(8,128)(2,1)}, bf16[256,512]{1,0:T(8,128)(2,1)}, bf16[256,512]{1,0:T(8,128)(2,1)}, bf16[256,512]{1,0:T(8,128)(2,1)}, f32[32,512]{1,0:T(8,128)}) custom-call(s32[32,64]{1,0:T(8,128)} %bitcast.6, s32[32,64]{1,0:T(8,128)} %bitcast.7, bf16[256,512]{1,0:T(8,128)(2,1)} %q_ref.1, bf16[2,128,512]{2,1,0:T(8,128)(2,1)} %bitcast.4, ...), custom_call_target="tpu_custom_call" | custom-call | tf_op jit(solution)/shard_map/pallas_call | solution.py:514
  81.9 2.2 %shard_map.111 = (bf16[256,512]{1,0:T(8,128)(2,1)}, bf16[256,512]{1,0:T(8,128)(2,1)}, bf16[256,512]{1,0:T(8,128)(2,1)}, bf16[256,512]{1,0:T(8,128)(2,1)}, f32[32,512]{1,0:T(8,128)}) custom-call(bf16[256,512]{1,0:T(8,128)(2,1)} %get-tuple-element.10.refs_0_, bf16[256,512]{1,0:T(8,128)(2,1)} %get-tuple-element.11.refs_1_, ...), custom_call_target="tpu_custom_call" | custom-call | tf_op jit(solution)/shard_map/pallas_call | solution.py:532

commit v6 on v4

--- a/solution.py
+++ b/solution.py
@@ -385,15 +385,21 @@
     for i in range(NY):
         pp[i] = pt[i].T.astype(BF16).reshape(NZ, NC, rows, DH)
         send(pp.at[i, :, 1 - c], rs0.at[i], bs.at[i], br.at[i], sibling)
-    for ry in range(NY):
+
+    def near_and_carry(ry):
         backward_near(ry)
         to = lax.rem(ry + NY - wrap, NY)
         send(carry_out.at[ry], carry_in.at[to], cs.at[ry], cr.at[to], back)
+
+    near_and_carry(0)
+    near_and_carry(1)
     for i in range(NY):
         arrived(rs0.at[i], bs.at[i], br.at[i])
         r1[:, i] = (pp[i, :, c].astype(F32) + rs0[i].astype(F32)).astype(BF16)
     for d in (4, 3, 5, 2, 6, 1, 7):
         send(r1.at[z_of[d]], rs2.at[d - 1], rzs.at[d - 1], rzr.at[d - 1], z_peer[d])
+    near_and_carry(2)
+    near_and_carry(3)
 
     for d in (1, 3, 2):
         arrived(attn_in.at[y_of[NY - d]], as_.at[d - 1], ar.at[d - 1])

time: 84.2 us -> 85.5 us (1.015)
  Pallas kernels: 83.3 us -> 84.6 us
    pallas_call x1, Pallas kernels: 81.2 us -> 82.4 us  [per_device(): pl.pallas_call(kernel, out_shape=shapes, in_specs=[vmem] * 2 + [anywhere]...]
where the time goes in v6:
time: 85.5 us; the launch traced here: 85.2 us
  Pallas kernels  84.6 us (99%)
    pallas_call x1, Pallas kernels, per_device(): pl.pallas_call(kernel, out_shape=shapes, in_specs=[vmem] * 2 + [anywhere]...  82.4 us
    pallas_call x1, Pallas kernels, per_device(): pl.pallas_call(hand_over, out_shape=shapes, in_specs=[vmem] * 5, out_spec...  2.18 us

profile of v6, /device:TPU:1, one launch (start us, length us, event | category | flops | bytes accessed | tf_op | source)
XLA Modules:
  0.0 85.2 jit_solution(17946667253755722520)
XLA Ops:
  0.6 82.4 %shard_map.110 = (bf16[256,512]{1,0:T(8,128)(2,1)}, bf16[256,512]{1,0:T(8,128)(2,1)}, bf16[256,512]{1,0:T(8,128)(2,1)}, bf16[256,512]{1,0:T(8,128)(2,1)}, f32[32,512]{1,0:T(8,128)}) custom-call(s32[32,64]{1,0:T(8,128)} %bitcast.6, s32[32,64]{1,0:T(8,128)} %bitcast.7, bf16[256,512]{1,0:T(8,128)(2,1)} %q_ref.1, bf16[2,128,512]{2,1,0:T(8,128)(2,1)} %bitcast.4, ...), custom_call_target="tpu_custom_call" | custom-call | tf_op jit(solution)/shard_map/pallas_call | solution.py:523
  83.0 2.2 %shard_map.111 = (bf16[256,512]{1,0:T(8,128)(2,1)}, bf16[256,512]{1,0:T(8,128)(2,1)}, bf16[256,512]{1,0:T(8,128)(2,1)}, bf16[256,512]{1,0:T(8,128)(2,1)}, f32[32,512]{1,0:T(8,128)}) custom-call(bf16[256,512]{1,0:T(8,128)(2,1)} %get-tuple-element.10.refs_0_, bf16[256,512]{1,0:T(8,128)(2,1)} %get-tuple-element.11.refs_1_, ...), custom_call_target="tpu_custom_call" | custom-call | tf_op jit(solution)/shard_map/pallas_call | solution.py:541
